TPU v7x, 128 devices: a whole 4x4x4 slice. The times are simulated.
128 devices in a mesh: gx: 8 (over z_hi, y), gy: 16 (over z_lo, x, core).
Axes of the slice: x: 4, y: 4, z: 4 (z_hi: 2, z_lo: 2; z = z_hi * 2 + z_lo), core: 2. Of those that a mesh axis runs over, the one named last changes fastest.
Arguments:
- tokens: bfloat16 [1024, 16384], P('gy', 'gx'), may hold values from -6 to 6
- gate_weight: bfloat16 [16384, 26624], P('gx', 'gy'), may hold values from -0.046875 to 0.046875
- up_weight: bfloat16 [16384, 26624], P('gx', 'gy'), may hold values from -0.046875 to 0.046875
- gate_scale: float32 [26624], P('gy'), may hold values from 0.5 to 2
- up_scale: float32 [26624], P('gy'), may hold values from 0.5 to 2
- down_weight: bfloat16 [26624, 16384], P('gy', 'gx'), may hold values from -0.0390625 to 0.0390625
- down_scale: float32 [16384], P('gx'), may hold values from 0.5 to 2
Outputs:
- mixed: bfloat16 [1024, 16384], P('gy', 'gx')
All inputs are finite; a program needn't handle non-finite values.
Results may differ from a plain program's by a relative error of at most 0.005.
Values may be sent and summed in bfloat16 or wider, within the bound.
A program may use at most 128 MiB of HBM per device.

v0:
```python
import jax
import jax.numpy as jnp
from jax import lax
from jax.sharding import PartitionSpec as P


def gated_rows(sums, gate_scale, up_scale):
    gate = sums[0] * gate_scale[None, :]
    up_value = sums[1] * up_scale[None, :]
    return (jax.nn.silu(gate) * up_value).astype(jnp.bfloat16)


def on_device(tokens, gate_weight, up_weight, gate_scale, up_scale, down_weight, down_scale):
    piece = lax.all_gather(tokens, "gy", axis=0, tiled=True)
    gate_term = jnp.dot(piece, gate_weight, preferred_element_type=jnp.float32)
    up_term = jnp.dot(piece, up_weight, preferred_element_type=jnp.float32)
    partial_value = jnp.stack([gate_term, up_term])
    totals = lax.psum(partial_value, "gx")
    hidden = gated_rows(totals, gate_scale, up_scale)
    terms = jnp.dot(hidden, down_weight, preferred_element_type=jnp.float32)
    summed = lax.psum_scatter(terms, "gy", scatter_dimension=0, tiled=True)
    return (summed * down_scale[None, :]).astype(jnp.bfloat16)


def solution(mesh):
    return jax.shard_map(
        on_device,
        mesh=mesh,
        in_specs=(
            P("gy", "gx"),
            P("gx", "gy"),
            P("gx", "gy"),
            P("gy"),
            P("gy"),
            P("gy", "gx"),
            P("gx"),
        ),
        out_specs=P("gy", "gx"),
        check_vma=False,
    )
```

profile of v0, /device:TPU:1, one launch (start us, length us, event | category | flops | bytes accessed | tf_op | source)
XLA Modules:
  0.0 464.3 jit_solution(18245453406323154992)
XLA Ops:
  6.5 0.0 all-gather.2.cloned.1.call-start
  6.5 0.7 all-gather.2.cloned.1.call-update
  7.3 0.0 all-reduce.2.cloned.1.call-start
  7.3 42.9 %all-gather.2.cloned.1.call-done = bf16[1024,2048]{1,0:T(8,128)(2,1)} async-done(((bf16[64,2048]{1,0:T(8,128)(2,1)}), bf16[1024,2048]{1,0:T(8,128)(2,1)}) %all-gather.2.cloned.1.call-update) | async-done | bytes 4194320 | tf_op jit(solution)/shard_map/all_gather | solution.py:14
  50.2 0.0 copy-start.1
  50.2 13.3 %convolution_bitcast_fusion = f32[1,1024,1664]{2,1,0:T(8,128)} fusion(bf16[1024,2048]{1,0:T(8,128)(2,1)} %all-gather.2.cloned.1.call-done, bf16[2048,1664]{1,0:T(8,128)(2,1)} %param.9), kind=kOutput, calls=%fused_computation.7 | convolution fusion | flops 6979321856 | bytes 17825792 | tf_op jit(solution)/shard_map/dot_general | solution.py:16
  63.5 0.0 copy-done.1
  63.5 12.7 %convolution_bitcast_fusion.1 = f32[1,1024,1664]{2,1,0:T(8,128)} fusion(bf16[1024,2048]{1,0:T(8,128)(2,1)S(1)} %copy-done.1, bf16[2048,1664]{1,0:T(8,128)(2,1)} %param.8), kind=kOutput, calls=%fused_computation.8 | convolution fusion | flops 6979321856 | bytes 17825792 | tf_op jit(solution)/shard_map/dot_general | solution.py:15
  76.2 10.6 %pad_maximum_fusion = f32[2,1024,1664]{2,1,0:T(8,128)} fusion(f32[1,1024,1664]{2,1,0:T(8,128)} %convolution_bitcast_fusion, f32[1,1024,1664]{2,1,0:T(8,128)} %convolution_bitcast_fusion.1), kind=kLoop, calls=%fused_computation | loop fusion | flops 3407872 | bytes 27262976 | tf_op jit(solution)/shard_map/stack | solution.py:17
  86.8 0.0 copy-start.2
  86.8 0.0 copy-start.3
  86.8 0.0 all-reduce.2.cloned.1.call-update
  86.9 0.0 reduce-scatter.2.cloned.1.call-start
  86.9 284.4 %all-reduce.2.cloned.1.call-done = f32[2,1024,1664]{2,1,0:T(8,128)} async-done(((f32[2,1024,1664]{2,1,0:T(8,128)}), f32[2,1024,1664]{2,1,0:T(8,128)}) %all-reduce.2.cloned.1.call-update) | async-done | bytes 13631504 | tf_op jit(solution)/shard_map/psum | solution.py:18
  371.3 0.0 copy-done.2
  371.3 0.0 copy-done.3
  371.3 16.3 %fusion.4 = f32[1024,2048]{1,0:T(8,128)} fusion(bf16[1664,2048]{1,0:T(8,128)(2,1)} %param.12, f32[2,1024,1664]{2,1,0:T(8,128)} %all-reduce.2.cloned.1.call-done, f32[1664]{0:T(1024)S(1)} %copy-done.2, f32[1664]{0:T(1024)S(1)} %copy-done.3), kind=kOutput, calls=%fused_computation.9 | convolution fusion | flops 6992953344 | bytes 28849152 | tf_op jit(solution)/shard_map/dot_general | solution.py:20
  387.6 0.0 copy-start
  387.6 0.0 reduce-scatter.2.cloned.1.call-update
  387.6 68.4 %reduce-scatter.2.cloned.1.call-done = f32[64,2048]{1,0:T(8,128)} async-done(((f32[1024,2048]{1,0:T(8,128)}), f32[64,2048]{1,0:T(8,128)}) %reduce-scatter.2.cloned.1.call-update) | async-done | bytes 524304 | tf_op jit(solution)/shard_map/reduce_scatter | solution.py:21
  456.0 0.0 copy-done
  456.0 1.8 multiply_convert_fusion
Async XLA Ops:
  6.5 43.7 %all-gather.2.cloned.1.call-start = ((), (), s32[]{:S(2)}) async-start(), calls=%async_computation.1 | async-start | bytes 4456448 | tf_op jit(solution)/shard_map/all_gather | solution.py:14
  7.3 364.1 %all-reduce.2.cloned.1.call-start = ((), (), s32[]{:S(2)}) async-start(), calls=%async_computation.2 | async-start | bytes 27262976 | tf_op jit(solution)/shard_map/psum | solution.py:18
  50.2 13.3 %copy-start.1 = (bf16[1024,2048]{1,0:T(8,128)(2,1)S(1)}, bf16[1024,2048]{1,0:T(8,128)(2,1)}, u32[]{:S(2)}) copy-start(bf16[1024,2048]{1,0:T(8,128)(2,1)} %all-gather.2.cloned.1.call-done) | copy-start | bytes 12582916
  86.8 284.5 %copy-start.2 = (f32[1664]{0:T(1024)S(1)}, f32[1664]{0:T(1024)}, u32[]{:S(2)}) copy-start(f32[1664]{0:T(1024)} %param.11) | copy-start | bytes 19972
  86.8 284.5 %copy-start.3 = (f32[1664]{0:T(1024)S(1)}, f32[1664]{0:T(1024)}, u32[]{:S(2)}) copy-start(f32[1664]{0:T(1024)} %param.10) | copy-start | bytes 19972
  86.9 369.1 %reduce-scatter.2.cloned.1.call-start = ((), (), s32[]{:S(2)}) async-start(), calls=%async_computation.3 | async-start | bytes 8912896 | tf_op jit(solution)/shard_map/reduce_scatter | solution.py:21
  387.6 68.4 %copy-start = (f32[2048]{0:T(1024)S(1)}, f32[2048]{0:T(1024)}, u32[]{:S(2)}) copy-start(f32[2048]{0:T(1024)} %param.13) | copy-start | bytes 24580
Sparse Core Ops, SparseCore 0:
  9.1 41.0 all-gather.1
  87.0 284.3 all-reduce.1
  387.7 68.1 reduce-scatter.1
where the time goes:
time: 468 us; the launch traced here: 464 us
  waiting for transfers between devices  396 us (85%)
  matrix products  42.3 us (9%)
  between operations  13.1 us (3%)
  other arithmetic  12.4 us (3%)
    psum x1, waiting for transfers between devices, on_device(): totals = lax.psum(partial_value, 'gx')  284 us
    reduce_scatter x1, waiting for transfers between devices, on_device(): summed = lax.psum_scatter(terms, 'gy', scatter_dimension=0, tiled=True)  68.4 us
    all_gather x1, waiting for transfers between devices, on_device(): piece = lax.all_gather(tokens, 'gy', axis=0, tiled=True)  42.9 us
    dot_general x1, matrix products, on_device(): terms = jnp.dot(hidden, down_weight, preferred_element_type=jnp.float32)  16.3 us
    dot_general x1, matrix products, on_device(): up_term = jnp.dot(piece, up_weight, preferred_element_type=jnp.float32)  13.3 us
    dot_general x1, matrix products, on_device(): gate_term = jnp.dot(piece, gate_weight, preferred_element_type=jnp.float32)  12.7 us
    another operation x1, other arithmetic, on_device(): partial_value = jnp.stack([gate_term, up_term])  10.6 us
  transfers between devices with their start and end apart: 3, of which 3 were waited for; matrix products, arithmetic and copies ran while one was open for 0% of the time, Pallas kernels for 0%

commit v1 on v0

v1 whole, which is shorter than its diff:
```python
import jax
import jax.numpy as jnp
from jax import lax
from jax.experimental import pallas as pl
from jax.experimental.pallas import tpu as pltpu
from jax.sharding import PartitionSpec as P

MESH = pl.DeviceIdType.MESH
BF, F32 = jnp.bfloat16, jnp.float32
NC = 8
K, N, N2, M = 2048, 1664, 3328, 2048
HALF = 896
LIFT = 2.0**50
TINY = 1e-37

S1P, S1M, S2P, S2M, S3P, S3M, ZS, HYP, HYM, HRP, HRM, HZ0, HZ1, HZ2, HZ3, CRS, XSN, TKF = range(18)
PER = 18
TOK = NC * PER
TK_CORE, TK_Z, TK_X, TK_ZX, ZLS = TOK, TOK + 1, TOK + 2, TOK + 5, TOK + 8
NSEM = TOK + 9

PIECES = ((0, 0, 1024, 0), (0, 1024, 640, 1024), (1, 0, 384, 1664), (1, 384, 1024, 2048), (1, 1408, 256, 3072))
W_FOR_TILE = ((0,), (1, 2), (3,), (4,))


def encode(v):
    v = v * LIFT
    return (v * jnp.abs(v)).astype(BF)


def decode(q):
    q = q.astype(F32)
    return q * lax.rsqrt(jnp.maximum(jnp.abs(q), TINY))


def recode(s):
    return (s * jnp.abs(s)).astype(BF)


def body(tok, wg, wu, gs, us, wd, ds, out, W, WD, T, PT, RL, RM, RP, ZR, H, D, CR, XS, XR, ACC, ZLB, ZLR, ssem, rsem, lsem):
    gx, gy = lax.axis_index("gx"), lax.axis_index("gy")
    zh, y = gx // 4, lax.rem(gx, 4)
    zl, x, core = gy // 8, lax.rem(gy // 2, 4), lax.rem(gy, 2)
    zo, other = 1 - zh, 1 - core
    yp, ym, y2 = lax.rem(y + 1, 4), lax.rem(y + 3, 4), lax.rem(y + 2, 4)

    def at(zh_=zh, y_=y, zl_=zl, x_=x, core_=core):
        return (zh_ * 4 + y_, zl_ * 8 + x_ * 2 + core_)

    to_yp, to_ym, to_zh, to_zl, to_core = at(y_=yp), at(y_=ym), at(zh_=zo), at(zl_=1 - zl), at(core_=other)
    xd = [lax.rem(x + d, 4) for d in range(4)]

    def own(y_, z_):
        return y_ * 2 + z_

    def copy(src, dst, k, to):
        return pltpu.make_async_remote_copy(
            src_ref=src, dst_ref=dst, send_sem=ssem.at[k], recv_sem=rsem.at[k], device_id=to, device_id_type=MESH
        )

    def arrived(dst, k):
        copy(dst, dst, k, to_core).wait_recv()

    def sent(src, k):
        copy(src, src, k, to_core).wait_send()

    w_copies = [
        pltpu.make_async_copy(
            (wg, wu)[m].at[:, pl.ds(c0, n)], W.at[:, pl.ds(d0, n)], lsem.at[i]
        )
        for i, (m, c0, n, d0) in enumerate(PIECES)
    ]
    own_copy = pltpu.make_async_copy(tok, T.at[0, core], lsem.at[5])
    wd_copy = pltpu.make_async_copy(wd, WD, lsem.at[6])
    own_copy.start()
    for c in w_copies:
        c.start()
    wd_copy.start()

    barrier = pltpu.get_barrier_semaphore()
    partners = [to_yp, to_ym, to_zh, to_zl, to_core] + [at(x_=xd[d]) for d in (1, 2, 3)]
    for p in partners:
        pl.semaphore_signal(barrier, inc=1, device_id=p, device_id_type=MESH)
    pl.semaphore_wait(barrier, len(partners))

    CHUNK = {(0, 0): 0, (0, 1): 1, (1, 1): 2, (3, 1): 3, (2, 1): 4, (2, 0): 5, (1, 0): 6, (3, 0): 7}

    def dx_of(c):
        return jnp.where((c == 2) | (c == 6), 1, jnp.where((c == 3) | (c == 7), 3, 2))

    copy(tok, T.at[0, core], TK_CORE, to_core).start()
    copy(tok, T.at[1, core], TK_Z, to_zl).start()
    for d in (2, 1, 3):
        copy(tok, T.at[CHUNK[((4 - d) % 4, 0)], core], TK_X + d - 1, at(x_=xd[d])).start()

    def recv_index(c):
        d = 4 - dx_of(c)
        return jnp.where(c == 1, TK_Z, jnp.where(c < 5, TK_ZX, TK_X) + d - 1)

    def forward_tokens(c):
        arrived(T.at[c, core], recv_index(c))
        copy(T.at[c, core], T.at[c, core], c * PER + TKF, to_core).start()

        @pl.when(c == 1)
        def _():
            for d in (1, 3, 2):
                copy(
                    T.at[1, core], T.at[CHUNK[((4 - d) % 4, 1)], core], TK_ZX + d - 1, at(x_=xd[d])
                ).start()

    def gate_up(c):
        @pl.when(c == 0)
        def _():
            own_copy.wait()
            arrived(T.at[0, other], TK_CORE)

        @pl.when(c > 0)
        def _():
            arrived(T.at[c, other], c * PER + TKF)

        def tile(n0, width):
            rows = T[c].reshape(128, K)
            part = jnp.dot(rows, W[:, pl.ds(n0, width)], preferred_element_type=F32)
            PT[c, :, :, pl.ds(n0, width)] = encode(part).reshape(8, 16, width)

        def step(n, carry):
            @pl.when(c == 0)
            def _():
                for t in range(3):

                    @pl.when(n == t)
                    def _():
                        for i in W_FOR_TILE[t]:
                            w_copies[i].wait()

            tile(pl.multiple_of(n * 1024, 1024), 1024)
            return carry

        lax.fori_loop(0, 3, step, 0)

        @pl.when(c == 0)
        def _():
            w_copies[4].wait()

        tile(3072, 256)
        b = c * PER
        copy(PT.at[c, own(y2, 0)], RL.at[c, 0], b + S1P, to_yp).start()
        copy(PT.at[c, own(y2, 1)], RL.at[c, 1], b + S1M, to_ym).start()
        copy(PT.at[c, own(yp, 1)], RM.at[c, 1], b + S2P, to_yp).start()
        copy(PT.at[c, own(ym, 0)], RP.at[c, 0], b + S2M, to_ym).start()

    def relay(c):
        b = c * PER
        arrived(RL.at[c, 0], b + S1P)
        o = own(yp, 0)
        PT[c, o] = recode(decode(PT[c, o]) + decode(RL[c, 0]))
        copy(PT.at[c, o], RM.at[c, 0], b + S3P, to_yp).start()
        arrived(RL.at[c, 1], b + S1M)
        o = own(ym, 1)
        PT[c, o] = recode(decode(PT[c, o]) + decode(RL[c, 1]))
        copy(PT.at[c, o], RP.at[c, 1], b + S3M, to_ym).start()

    def over_y(c):
        b = c * PER
        arrived(RM.at[c, 1], b + S2P)
        arrived(RP.at[c, 0], b + S2M)
        arrived(RM.at[c, 0], b + S3P)
        arrived(RP.at[c, 1], b + S3M)
        o = own(y, zo)
        PT[c, o] = recode(decode(PT[c, o]) + decode(RM[c, zo]) + decode(RP[c, zo]))
        copy(PT.at[c, o], ZR.at[c], b + ZS, to_zh).start()

    def hidden_rows(c):
        b = c * PER
        arrived(ZR.at[c], b + ZS)
        o = own(y, zh)

        def total(cols):
            return (
                decode(PT[c, o, :, cols]) + decode(RM[c, zh, :, cols])
                + decode(RP[c, zh, :, cols]) + decode(ZR[c, :, cols])
            )

        gate = total(pl.ds(0, N)) * (gs[...] * (1.0 / LIFT))[None, :]
        up = total(pl.ds(N, N)) * (us[...] * (1.0 / LIFT))[None, :]
        H[c, o] = (jax.nn.silu(gate) * up).astype(BF)
        copy(H.at[c, o], H.at[c, o], b + HYP, to_yp).start()
        copy(H.at[c, o], H.at[c, o], b + HYM, to_ym).start()
        copy(H.at[c, o], H.at[c, o], b + HZ0, to_zh).start()

    def near_rows(c):
        b = c * PER
        om, op = own(ym, zh), own(yp, zh)
        arrived(H.at[c, om], b + HYP)
        left = H.at[c, om, :, pl.ds(0, HALF)]
        copy(left, left, b + HRP, to_yp).start()
        copy(H.at[c, om], H.at[c, om], b + HZ1, to_zh).start()
        arrived(H.at[c, op], b + HYM)
        right = H.at[c, op, :, pl.ds(HALF, N - HALF)]
        copy(right, right, b + HRM, to_ym).start()
        copy(H.at[c, op], H.at[c, op], b + HZ2, to_zh).start()

    def far_rows(c):
        b = c * PER
        o = own(y2, zh)
        arrived(H.at[c, o, :, pl.ds(0, HALF)], b + HRP)
        arrived(H.at[c, o, :, pl.ds(HALF, N - HALF)], b + HRM)
        copy(H.at[c, o], H.at[c, o], b + HZ3, to_zh).start()

    def down(c):
        b = c * PER
        arrived(H.at[c, own(y, zo)], b + HZ0)
        arrived(H.at[c, own(ym, zo)], b + HZ1)
        arrived(H.at[c, own(yp, zo)], b + HZ2)
        arrived(H.at[c, own(y2, zo)], b + HZ3)
        slot = lax.rem(c, 2)

        @pl.when(c == 0)
        def _():
            wd_copy.wait()

        @pl.when(c >= 2)
        def _():
            sent(D.at[slot, other], (c - 2) * PER + CRS)

        def step(n, carry):
            cols = pl.ds(pl.multiple_of(n * 1024, 1024), 1024)
            rows = H[c].reshape(128, N)
            D[slot, :, :, cols] = jnp.dot(rows, WD[:, cols], preferred_element_type=F32).reshape(2, 64, 1024)
            return carry

        lax.fori_loop(0, 2, step, 0)
        copy(D.at[slot, other], CR.at[c], b + CRS, to_core).start()

    def over_core(c):
        b = c * PER
        slot = lax.rem(c, 2)
        arrived(CR.at[c], b + CRS)

        @pl.when(c < 2)
        def _():
            ACC[c] = D[slot, core] + CR[c]

        @pl.when(c >= 2)
        def _():
            XS[c - 2] = (D[slot, core] + CR[c]).astype(BF)
            copy(XS.at[c - 2], XR.at[c - 2], b + XSN, at(x_=lax.rem(x + dx_of(c), 4))).start()

    def over_x(first, a):
        for c in range(first, first + 3):
            arrived(XR.at[c - 2], c * PER + XSN)
        return ACC[a] + (XR[first - 2].astype(F32) + XR[first - 1].astype(F32) + XR[first].astype(F32))

    def for_partner():
        ZLB[...] = over_x(2, 1).astype(BF)
        copy(ZLB, ZLR, ZLS, to_zl).start()

    plan = (
        (gate_up, 0),
        (forward_tokens, -1),
        (hidden_rows, 2),
        (far_rows, 3),
        (over_y, 1),
        (down, 4),
        (over_core, 5),
        (near_rows, 2),
        (relay, 0),
    )

    def step(s, carry):
        for task, lag in plan:
            c = s - lag

            @pl.when((c >= (1 if task is forward_tokens else 0)) & (c < NC))
            def _():
                task(c)

            if task is down:

                @pl.when(s == 11)
                def _():
                    for_partner()

        return carry

    lax.fori_loop(0, NC + 5, step, 0)

    near = over_x(5, 0)
    arrived(ZLR, ZLS)
    out[...] = ((near + ZLR[...].astype(F32)) * ds[...][None, :]).astype(BF)

    def drain(c, carry):
        b = c * PER
        for k in (S1P, S1M, S2P, S2M, S3P, S3M, ZS):
            sent(PT.at[c, 0], b + k)
        for k in (HYP, HYM, HZ0, HZ1, HZ2, HZ3):
            sent(H.at[c, 0], b + k)
        sent(H.at[c, 0, :, pl.ds(0, HALF)], b + HRP)
        sent(H.at[c, 0, :, pl.ds(HALF, N - HALF)], b + HRM)

        @pl.when(c >= NC - 2)
        def _():
            sent(D.at[0, 0], b + CRS)

        @pl.when(c >= 2)
        def _():
            sent(XS.at[0], b + XSN)

        @pl.when(c >= 1)
        def _():
            sent(T.at[c, core], b + TKF)

        return carry

    lax.fori_loop(0, NC, drain, 0)
    for k in range(TK_CORE, TK_CORE + 8):
        sent(T.at[0, core], k)
    sent(ZLB, ZLS)


def on_device(tokens, gate_weight, up_weight, gate_scale, up_scale, down_weight, down_scale):
    hbm, vmem = pl.BlockSpec(memory_space=pl.ANY), pl.BlockSpec(memory_space=pltpu.VMEM)
    return pl.pallas_call(
        body,
        name="gated_layer",
        out_shape=jax.ShapeDtypeStruct((64, M), BF),
        in_specs=[hbm, hbm, hbm, vmem, vmem, hbm, vmem],
        out_specs=vmem,
        scratch_shapes=[
            pltpu.VMEM((K, N2), BF),
            pltpu.VMEM((N, M), BF),
            pltpu.VMEM((NC, 2, 64, K), BF),
            pltpu.VMEM((NC, 8, 16, N2), BF),
            pltpu.VMEM((NC, 2, 16, N2), BF),
            pltpu.VMEM((NC, 2, 16, N2), BF),
            pltpu.VMEM((NC, 2, 16, N2), BF),
            pltpu.VMEM((NC, 16, N2), BF),
            pltpu.VMEM((NC, 8, 16, N), BF),
            pltpu.VMEM((2, 2, 64, M), F32),
            pltpu.VMEM((NC, 64, M), F32),
            pltpu.VMEM((6, 64, M), BF),
            pltpu.VMEM((6, 64, M), BF),
            pltpu.VMEM((2, 64, M), F32),
            pltpu.VMEM((64, M), BF),
            pltpu.VMEM((64, M), BF),
            pltpu.SemaphoreType.DMA((NSEM,)),
            pltpu.SemaphoreType.DMA((NSEM,)),
            pltpu.SemaphoreType.DMA((7,)),
        ],
        compiler_params=pltpu.CompilerParams(
            collective_id=0, has_side_effects=True, vmem_limit_bytes=62 * 2**20
        ),
        cost_estimate=pl.CostEstimate(
            flops=2 * 1024 * K * N2 + 2 * 1024 * N * M, bytes_accessed=2 * (K * N2 + N * M), transcendentals=0
        ),
    )(tokens, gate_weight, up_weight, gate_scale, up_scale, down_weight, down_scale)


def solution(mesh):
    return jax.shard_map(
        on_device,
        mesh=mesh,
        in_specs=(
            P("gy", "gx"),
            P("gx", "gy"),
            P("gx", "gy"),
            P("gy"),
            P("gy"),
            P("gy", "gx"),
            P("gx"),
        ),
        out_specs=P("gy", "gx"),
        check_vma=False,
    )
```

time: 468 us -> 128 us (0.27)
  waiting for transfers between devices: 396 us -> 0 us
  Pallas kernels: 0 us -> 126 us
  matrix products: 42.3 us -> 0 us
  between operations: 13.1 us -> 0.01 us
  other arithmetic: 12.4 us -> 0 us
    psum x1 -> x0, waiting for transfers between devices: 284 us -> none  [on_device(): totals = lax.psum(partial_value, 'gx')]
    pallas_call x0 -> x1, Pallas kernels: none -> 126 us  [on_device(): pl.pallas_call(body, name='gated_layer', out_shape=jax.ShapeDtypeStruct((...]
    reduce_scatter x1 -> x0, waiting for transfers between devices: 68.4 us -> none  [on_device(): summed = lax.psum_scatter(terms, 'gy', scatter_dimension=0, tiled=True)]
    all_gather x1 -> x0, waiting for transfers between devices: 42.9 us -> none  [on_device(): piece = lax.all_gather(tokens, 'gy', axis=0, tiled=True)]
    dot_general x3 -> x0, matrix products: 42.3 us -> none  [the longest x1 16.3 us: on_device(): terms = jnp.dot(hidden, down_weight, preferred_element_type=jnp.float32)]
    another operation x1 -> x0, other arithmetic: 10.6 us -> none  [on_device(): partial_value = jnp.stack([gate_term, up_term])]
  transfers between devices with their start and end apart: 3 -> 0, of which waited for: 3 -> 0; matrix products, arithmetic and copies ran while one was open for 0% -> 0% of each run, Pallas kernels for 0% -> 0%
where the time goes in v1:
time: 128 us
  Pallas kernels  126 us (98%)
  local copies, waits for them, and re-layouts  1.67 us (1%)
    pallas_call x1, Pallas kernels, on_device(): pl.pallas_call(body, name='gated_layer', out_shape=jax.ShapeDtypeStruct((...  126 us

profile of v1, /device:TPU:1, one launch (start us, length us, event | category | flops | bytes accessed | tf_op | source)
XLA Modules:
  0.0 127.6 jit_solution(5434403331397952119)
XLA Ops:
  0.0 126.0 %gated_layer.1 = bf16[64,2048]{1,0:T(8,128)(2,1)} custom-call(bf16[64,2048]{1,0:T(8,128)(2,1)} %tok.1, bf16[2048,1664]{1,0:T(8,128)(2,1)} %wg.1, bf16[2048,1664]{1,0:T(8,128)(2,1)} %wu.1, f32[1664]{0:T(1024)} %gs.1, f32[1664]{0:T(1024)} %us.1, bf16[1664,2048]{1,0:T(8,128)(2,1)} %wd.1, f32[2048]{0:T(1024)} %ds.1), custom_call_target="tpu_custom_call" | custom-call | flops 20937965568 | bytes 20447232 | tf_op jit(solution)/shard_map/gated_layer/pallas_call | solution.py:323
  126.0 1.7 %copy.9 = bf16[64,2048]{1,0:T(8,128)(2,1)} copy(bf16[64,2048]{1,0:T(8,128)(2,1)} %gated_layer.1) | data formatting | bytes 524288

commit v2 on v0

v2 whole, which is shorter than its diff:
```python
import jax
import jax.numpy as jnp
from jax import lax
from jax.experimental import pallas as pl
from jax.experimental.pallas import tpu as pltpu
from jax.sharding import PartitionSpec as P

MESH = pl.DeviceIdType.MESH
BF, F32 = jnp.bfloat16, jnp.float32
NC = 8
K, N, N2, M = 2048, 1664, 3328, 2048
HALF = 896
LIFT = 2.0**50
TINY = 1e-37

CHUNKS = ("own", "x2", "z", "zx2", "zx1", "zx3", "mixA", "mixB")
DIRECT = (7,)
SPLIT = (7,)
ORDER = (
    ("send_far", 0), ("gate_up", 0), ("forward", 1), ("forward", 2), ("relay", 0), ("gate_up", 1), ("gate_up", 2),
    ("forward", 4), ("send_near", 0), ("over_y", 0), ("relay", 1), ("forward", 3), ("hidden", 0), ("relay", 2),
    ("forward", 5), ("forward", 6), ("gate_up", 3), ("over_y", 1), ("near", 0), ("hidden", 1), ("over_y", 2),
    ("relay", 3), ("gate_up", 4), ("far", 0), ("hidden", 2), ("near", 1), ("over_y", 3), ("gate_up", 5), ("far", 1),
    ("down", 0), ("forward", 7), ("relay", 5), ("relay", 4), ("hidden", 3), ("near", 2), ("gate_up", 6),
    ("over_y", 5), ("down", 1), ("over_y", 4), ("near", 3), ("far", 2), ("relay", 6), ("hidden", 5), ("hidden", 4),
    ("gate_up", 7), ("far", 3), ("over_core", 1), ("over_y", 6), ("near", 4), ("over_core", 0), ("near", 5),
    ("down", 2), ("relay", 7), ("down", 3), ("far", 4), ("far", 5), ("hidden", 6), ("over_core", 2), ("over_core", 3),
    ("over_y", 7), ("down", 4), ("down", 5), ("near", 6), ("far", 6), ("over_core", 4), ("over_core", 5),
    ("hidden", 7), ("down", 6), ("over_core", 6), ("partner", 0), ("down_a", 7), ("down_b", 7), ("over_core_a", 7),
    ("over_core_b", 7),
)

ALONG_X = {"x2": (2,), "zx1": (1,), "zx2": (2,), "zx3": (3,), "mixA": (1, 3), "mixB": (1, 3)}
PIECES = ((0, 0, 1024, 0), (0, 1024, 640, 1024), (1, 0, 384, 1664), (1, 384, 1024, 2048), (1, 1408, 256, 3072))
W_FOR_TILE = ((0,), (1, 2), (3,), (4,))
NSEM = 176


def encode(v):
    v = v * LIFT
    return (v * jnp.abs(v)).astype(BF)


def decode(q):
    q = q.astype(F32)
    return q * lax.rsqrt(jnp.maximum(jnp.abs(q), TINY))


def recode(s):
    return (s * jnp.abs(s)).astype(BF)


def body(tok, wg, wu, gs, us, wd, ds, out, W, WD, T, PT, RL, RM, RP, ZR, H, D, CR, XS, XR, ACC, ZLB, ZLR, ssem, rsem, lsem):
    gx, gy = lax.axis_index("gx"), lax.axis_index("gy")
    zh, y = gx // 4, lax.rem(gx, 4)
    zl, x, core = gy // 8, lax.rem(gy // 2, 4), lax.rem(gy, 2)
    zo, other = 1 - zh, 1 - core
    yp, ym, y2 = lax.rem(y + 1, 4), lax.rem(y + 3, 4), lax.rem(y + 2, 4)

    def at(zh_=zh, y_=y, zl_=zl, x_=x, core_=core):
        return (zh_ * 4 + y_, zl_ * 8 + x_ * 2 + core_)

    to_yp, to_ym, to_y2 = at(y_=yp), at(y_=ym), at(y_=y2)
    to_zh, to_zh_yp, to_zh_ym, to_zh_y2 = at(zh_=zo), at(zh_=zo, y_=yp), at(zh_=zo, y_=ym), at(zh_=zo, y_=y2)
    to_zl, to_core = at(zl_=1 - zl), at(core_=other)
    to_x = [None] + [at(x_=lax.rem(x + d, 4)) for d in (1, 2, 3)]

    def own(y_, z_):
        return y_ * 2 + z_

    semaphore, on_way = {}, {}

    def copy(src, dst, key, to):
        k = semaphore.setdefault(key, len(semaphore))
        return pltpu.make_async_remote_copy(
            src_ref=src, dst_ref=dst, send_sem=ssem.at[k], recv_sem=rsem.at[k], device_id=to, device_id_type=MESH
        )

    def send(src, dst, key, to):
        on_way[key] = copy(src, dst, key, to)
        on_way[key].start()

    def arrived(dst, key):
        copy(dst, dst, key, to_core).wait_recv()

    w_copies = [
        pltpu.make_async_copy((wg, wu)[m].at[:, pl.ds(c0, n)], W.at[:, pl.ds(d0, n)], lsem.at[i])
        for i, (m, c0, n, d0) in enumerate(PIECES)
    ]
    own_copy = pltpu.make_async_copy(tok, T.at[CHUNKS.index("own"), core], lsem.at[5])
    wd_copy = pltpu.make_async_copy(wd, WD, lsem.at[6])
    own_copy.start()
    for c in w_copies:
        c.start()

    barrier = pltpu.get_barrier_semaphore()
    partners = [to_yp, to_ym, to_y2, to_zh, to_zh_yp, to_zh_ym, to_zh_y2, to_zl, to_core] + to_x[1:]
    for p in partners:
        pl.semaphore_signal(barrier, inc=1, device_id=p, device_id_type=MESH)
    pl.semaphore_wait(barrier, len(partners))

    def chunk_tokens(c):
        name = CHUNKS[c]
        if name[:3] == "mix":
            return [(T.at[c, core, pl.ds(32 * i, 32)], ("tok", name, d)) for i, d in enumerate((1, 3))]
        return [(T.at[c, core], ("tok", name))]

    def send_far(_):
        send(tok, T.at[CHUNKS.index("x2"), core], ("tok", "x2"), to_x[2])

    def send_near(_):
        for i, name in enumerate(("mixA", "mixB")):
            c = CHUNKS.index(name)
            rows = tok.at[pl.ds(32 * i, 32)]
            send(rows, T.at[c, core, pl.ds(32, 32)], ("tok", name, 3), to_x[1])
            send(rows, T.at[c, core, pl.ds(0, 32)], ("tok", name, 1), to_x[3])

    def forward(c):
        for where, key in chunk_tokens(c):
            arrived(where, key)
        send(T.at[c, core], T.at[c, core], ("fwd", c), to_core)
        if CHUNKS[c] == "z":
            for d in (1, 3, 2):
                name = "zx%d" % (4 - d)
                send(T.at[c, core], T.at[CHUNKS.index(name), core], ("tok", name), to_x[d])

    def gate_up(c):
        if CHUNKS[c] == "own":
            own_copy.wait()
        arrived(T.at[c, other], ("fwd", c))

        def tile(n0, width):
            rows = T[c].reshape(128, K)
            part = jnp.dot(rows, W[:, pl.ds(n0, width)], preferred_element_type=F32)
            PT[c, :, :, pl.ds(n0, width)] = encode(part).reshape(8, 16, width)

        def step(n, carry):
            if c == 0:
                for t in range(3):

                    @pl.when(n == t)
                    def _():
                        for i in W_FOR_TILE[t]:
                            w_copies[i].wait()

            tile(pl.multiple_of(n * 1024, 1024), 1024)
            return carry

        lax.fori_loop(0, 3, step, 0)
        if c == 0:
            w_copies[4].wait()
        tile(3072, 256)
        send(PT.at[c, own(y2, 0)], RL.at[c, 0], ("far+", c), to_yp)
        send(PT.at[c, own(y2, 1)], RL.at[c, 1], ("far-", c), to_ym)
        send(PT.at[c, own(yp, 1)], RM.at[c, 1], ("near+", c), to_yp)
        send(PT.at[c, own(ym, 0)], RP.at[c, 0], ("near-", c), to_ym)
        if c == 0:
            wd_copy.start()

    def relay(c):
        arrived(RL.at[c, 0], ("far+", c))
        o = own(yp, 0)
        PT[c, o] = recode(decode(PT[c, o]) + decode(RL[c, 0]))
        send(PT.at[c, o], RM.at[c, 0], ("via+", c), to_yp)
        arrived(RL.at[c, 1], ("far-", c))
        o = own(ym, 1)
        PT[c, o] = recode(decode(PT[c, o]) + decode(RL[c, 1]))
        send(PT.at[c, o], RP.at[c, 1], ("via-", c), to_ym)

    def over_y(c):
        arrived(RM.at[c, 1], ("near+", c))
        arrived(RP.at[c, 0], ("near-", c))
        arrived(RM.at[c, 0], ("via+", c))
        arrived(RP.at[c, 1], ("via-", c))
        o = own(y, zo)
        PT[c, o] = recode(decode(PT[c, o]) + decode(RM[c, zo]) + decode(RP[c, zo]))
        send(PT.at[c, o], ZR.at[c], ("z_hi", c), to_zh)

    def hidden(c):
        arrived(ZR.at[c], ("z_hi", c))
        o = own(y, zh)

        def total(cols):
            return (
                decode(PT[c, o, :, cols]) + decode(RM[c, zh, :, cols])
                + decode(RP[c, zh, :, cols]) + decode(ZR[c, :, cols])
            )

        gate = total(pl.ds(0, N)) * (gs[...] * (1.0 / LIFT))[None, :]
        up = total(pl.ds(N, N)) * (us[...] * (1.0 / LIFT))[None, :]
        H[c, o] = (jax.nn.silu(gate) * up).astype(BF)
        rows = H.at[c, o]
        send(rows, rows, ("h+", c), to_yp)
        send(rows, rows, ("h-", c), to_ym)
        send(rows, rows, ("hz", c), to_zh)
        if c in DIRECT:
            send(rows, rows, ("hz+", c), to_zh_yp)
            send(rows, rows, ("hz-", c), to_zh_ym)
            send(rows, rows, ("h2", c), to_y2)
            send(rows, rows, ("hz2", c), to_zh_y2)

    def near(c):
        rows = H.at[c, own(ym, zh)]
        arrived(rows, ("h+", c))
        left = rows.at[:, pl.ds(0, HALF)]
        send(left, left, ("hv+", c), to_yp)
        send(rows, rows, ("hz+", c), to_zh)
        rows = H.at[c, own(yp, zh)]
        arrived(rows, ("h-", c))
        right = rows.at[:, pl.ds(HALF, N - HALF)]
        send(right, right, ("hv-", c), to_ym)
        send(rows, rows, ("hz-", c), to_zh)

    def far(c):
        rows = H.at[c, own(y2, zh)]
        arrived(rows.at[:, pl.ds(0, HALF)], ("hv+", c))
        arrived(rows.at[:, pl.ds(HALF, N - HALF)], ("hv-", c))
        send(rows, rows, ("hz2", c), to_zh)

    def down_tile(c, n):
        cols = pl.ds(n * 1024, 1024) if isinstance(n, int) else pl.ds(pl.multiple_of(n * 1024, 1024), 1024)
        rows = H[c].reshape(128, N)
        part = jnp.dot(rows, WD[:, cols], preferred_element_type=F32)
        D[c % 2, :, :, cols] = part.reshape(2, 64, 1024)

    def before_down(c):
        if c in DIRECT:
            arrived(H.at[c, own(ym, zh)], ("h+", c))
            arrived(H.at[c, own(yp, zh)], ("h-", c))
            arrived(H.at[c, own(y2, zh)], ("h2", c))
        arrived(H.at[c, own(y, zo)], ("hz", c))
        arrived(H.at[c, own(ym, zo)], ("hz+", c))
        arrived(H.at[c, own(yp, zo)], ("hz-", c))
        arrived(H.at[c, own(y2, zo)], ("hz2", c))
        if c == 0:
            wd_copy.wait()
        if c >= 2:
            on_way.pop(("core", c - 2)).wait_send()

    def down(c):
        before_down(c)

        def step(n, carry):
            down_tile(c, n)
            return carry

        lax.fori_loop(0, 2, step, 0)
        send(D.at[c % 2, other], CR.at[c], ("core", c), to_core)

    def down_part(c, n):
        if n == 0:
            before_down(c)
        down_tile(c, n)
        cols = pl.ds(n * 1024, 1024)
        send(D.at[c % 2, other, :, cols], CR.at[c, :, cols], ("core", c, n), to_core)

    def add_cores(c, cols, tag):
        name = CHUNKS[c]
        arrived(CR.at[c, :, cols], ("core", c) + tag)
        total = D[c % 2, core, :, cols] + CR[c, :, cols]
        if name not in ALONG_X:
            ACC[("own", "z").index(name), :, cols] = total
            return
        XS[c, :, cols] = total.astype(BF)
        ways = ALONG_X[name]
        rows = 64 // len(ways)
        for i, d in enumerate(ways):
            part = pl.ds(i * rows, rows)
            send(XS.at[c, part, cols], XR.at[c, part, cols], ("x", c, i) + tag, to_x[d])

    def over_core(c):
        add_cores(c, pl.ds(0, M), ())

    def sums_arrived(c):
        ways = ALONG_X[CHUNKS[c]]
        rows = 64 // len(ways)
        for i in range(len(ways)):
            part = pl.ds(i * rows, rows)
            if c in SPLIT:
                for n in range(2):
                    cols = pl.ds(n * 1024, 1024)
                    arrived(XR.at[c, part, cols], ("x", c, i, n))
            else:
                arrived(XR.at[c, part], ("x", c, i))

    def partner(_):
        total = ACC[1]
        for name in ("zx1", "zx2", "zx3"):
            c = CHUNKS.index(name)
            sums_arrived(c)
            total = total + XR[c].astype(F32)
        ZLB[...] = total.astype(BF)
        send(ZLB, ZLR, ("z_lo",), to_zl)

    own_key, z_key = ("fwd", CHUNKS.index("own")), ("tok", "z")
    send(tok, T.at[CHUNKS.index("own"), core], own_key, to_core)
    send(tok, T.at[CHUNKS.index("z"), core], z_key, to_zl)

    steps = dict(
        send_far=send_far, send_near=send_near, forward=forward, gate_up=gate_up, relay=relay, over_y=over_y,
        hidden=hidden, near=near, far=far, down=down, over_core=over_core, partner=partner,
        down_a=lambda c: down_part(c, 0), down_b=lambda c: down_part(c, 1),
        over_core_a=lambda c: add_cores(c, pl.ds(0, 1024), (0,)),
        over_core_b=lambda c: add_cores(c, pl.ds(1024, 1024), (1,)),
    )
    for name, c in ORDER:
        steps[name](c)

    c2, ca, cb = CHUNKS.index("x2"), CHUNKS.index("mixA"), CHUNKS.index("mixB")
    sums_arrived(c2)
    base = ACC[0] + XR[c2].astype(F32)
    arrived(ZLR, ("z_lo",))
    base = base + ZLR[...].astype(F32)
    for i, c in enumerate((ca, cb)):
        sums_arrived(c)
        rows = slice(32 * i, 32 * i + 32)
        total = base[rows] + XR[c, 0:32].astype(F32) + XR[c, 32:64].astype(F32)
        out[rows, :] = (total * ds[...][None, :]).astype(BF)

    for c in on_way.values():
        c.wait_send()


def on_device(tokens, gate_weight, up_weight, gate_scale, up_scale, down_weight, down_scale):
    hbm, vmem = pl.BlockSpec(memory_space=pl.ANY), pl.BlockSpec(memory_space=pltpu.VMEM)
    return pl.pallas_call(
        body,
        name="gated_layer",
        out_shape=jax.ShapeDtypeStruct((64, M), BF),
        in_specs=[hbm, hbm, hbm, vmem, vmem, hbm, vmem],
        out_specs=vmem,
        scratch_shapes=[
            pltpu.VMEM((K, N2), BF),
            pltpu.VMEM((N, M), BF),
            pltpu.VMEM((NC, 2, 64, K), BF),
            pltpu.VMEM((NC, 8, 16, N2), BF),
            pltpu.VMEM((NC, 2, 16, N2), BF),
            pltpu.VMEM((NC, 2, 16, N2), BF),
            pltpu.VMEM((NC, 2, 16, N2), BF),
            pltpu.VMEM((NC, 16, N2), BF),
            pltpu.VMEM((NC, 8, 16, N), BF),
            pltpu.VMEM((2, 2, 64, M), F32),
            pltpu.VMEM((NC, 64, M), F32),
            pltpu.VMEM((NC, 64, M), BF),
            pltpu.VMEM((NC, 64, M), BF),
            pltpu.VMEM((2, 64, M), F32),
            pltpu.VMEM((64, M), BF),
            pltpu.VMEM((64, M), BF),
            pltpu.SemaphoreType.DMA((NSEM,)),
            pltpu.SemaphoreType.DMA((NSEM,)),
            pltpu.SemaphoreType.DMA((7,)),
        ],
        compiler_params=pltpu.CompilerParams(
            collective_id=0, has_side_effects=True, vmem_limit_bytes=62 * 2**20
        ),
        cost_estimate=pl.CostEstimate(
            flops=2 * 1024 * K * N2 + 2 * 1024 * N * M, bytes_accessed=2 * (K * N2 + N * M), transcendentals=0
        ),
    )(tokens, gate_weight, up_weight, gate_scale, up_scale, down_weight, down_scale)


def solution(mesh):
    return jax.shard_map(
        on_device,
        mesh=mesh,
        in_specs=(
            P("gy", "gx"),
            P("gx", "gy"),
            P("gx", "gy"),
            P("gy"),
            P("gy"),
            P("gy", "gx"),
            P("gx"),
        ),
        out_specs=P("gy", "gx"),
        check_vma=False,
    )
```

time: 468 us -> 111 us (0.24)
  waiting for transfers between devices: 396 us -> 0 us
  Pallas kernels: 0 us -> 110 us
  matrix products: 42.3 us -> 0 us
  between operations: 13.1 us -> 0.01 us
  other arithmetic: 12.4 us -> 0 us
    psum x1 -> x0, waiting for transfers between devices: 284 us -> none  [on_device(): totals = lax.psum(partial_value, 'gx')]
    pallas_call x0 -> x1, Pallas kernels: none -> 110 us  [on_device(): pl.pallas_call(body, name='gated_layer', out_shape=jax.ShapeDtypeStruct((...]
    reduce_scatter x1 -> x0, waiting for transfers between devices: 68.4 us -> none  [on_device(): summed = lax.psum_scatter(terms, 'gy', scatter_dimension=0, tiled=True)]
    all_gather x1 -> x0, waiting for transfers between devices: 42.9 us -> none  [on_device(): piece = lax.all_gather(tokens, 'gy', axis=0, tiled=True)]
    dot_general x3 -> x0, matrix products: 42.3 us -> none  [the longest x1 16.3 us: on_device(): terms = jnp.dot(hidden, down_weight, preferred_element_type=jnp.float32)]
    another operation x1 -> x0, other arithmetic: 10.6 us -> none  [on_device(): partial_value = jnp.stack([gate_term, up_term])]
  transfers between devices with their start and end apart: 3 -> 0, of which waited for: 3 -> 0; matrix products, arithmetic and copies ran while one was open for 0% -> 0% of each run, Pallas kernels for 0% -> 0%
where the time goes in v2:
time: 111 us
  Pallas kernels  110 us (99%)
  local copies, waits for them, and re-layouts  1.67 us (2%)
    pallas_call x1, Pallas kernels, on_device(): pl.pallas_call(body, name='gated_layer', out_shape=jax.ShapeDtypeStruct((...  110 us

profile of v2, /device:TPU:1, one launch (start us, length us, event | category | flops | bytes accessed | tf_op | source)
XLA Modules:
  0.0 111.2 jit_solution(17856227117692449582)
XLA Ops:
  0.0 109.5 %gated_layer.1 = bf16[64,2048]{1,0:T(8,128)(2,1)} custom-call(bf16[64,2048]{1,0:T(8,128)(2,1)} %tok.1, bf16[2048,1664]{1,0:T(8,128)(2,1)} %wg.1, bf16[2048,1664]{1,0:T(8,128)(2,1)} %wu.1, f32[1664]{0:T(1024)} %gs.1, f32[1664]{0:T(1024)} %us.1, bf16[1664,2048]{1,0:T(8,128)(2,1)} %wd.1, f32[2048]{0:T(1024)} %ds.1), custom_call_target="tpu_custom_call" | custom-call | flops 20937965568 | bytes 20447232 | tf_op jit(solution)/shard_map/gated_layer/pallas_call | solution.py:326
  109.5 1.7 %copy.9 = bf16[64,2048]{1,0:T(8,128)(2,1)} copy(bf16[64,2048]{1,0:T(8,128)(2,1)} %gated_layer.1) | data formatting | bytes 524288

commit v3 on v2

--- a/solution.py
+++ b/solution.py
@@ -14,26 +14,43 @@
 TINY = 1e-37
 
 CHUNKS = ("own", "x2", "z", "zx2", "zx1", "zx3", "mixA", "mixB")
-DIRECT = (7,)
-SPLIT = (7,)
+DIRECT = (6, 7)
+SPLIT = (6, 7)
+RS_GROUPS = (0, 6, 7)
 ORDER = (
-    ("send_far", 0), ("gate_up", 0), ("forward", 1), ("forward", 2), ("relay", 0), ("gate_up", 1), ("gate_up", 2),
-    ("forward", 4), ("send_near", 0), ("over_y", 0), ("relay", 1), ("forward", 3), ("hidden", 0), ("relay", 2),
-    ("forward", 5), ("forward", 6), ("gate_up", 3), ("over_y", 1), ("near", 0), ("hidden", 1), ("over_y", 2),
-    ("relay", 3), ("gate_up", 4), ("far", 0), ("hidden", 2), ("near", 1), ("over_y", 3), ("gate_up", 5), ("far", 1),
-    ("down", 0), ("forward", 7), ("relay", 5), ("relay", 4), ("hidden", 3), ("near", 2), ("gate_up", 6),
-    ("over_y", 5), ("down", 1), ("over_y", 4), ("near", 3), ("far", 2), ("relay", 6), ("hidden", 5), ("hidden", 4),
-    ("gate_up", 7), ("far", 3), ("over_core", 1), ("over_y", 6), ("near", 4), ("over_core", 0), ("near", 5),
-    ("down", 2), ("relay", 7), ("down", 3), ("far", 4), ("far", 5), ("hidden", 6), ("over_core", 2), ("over_core", 3),
-    ("over_y", 7), ("down", 4), ("down", 5), ("near", 6), ("far", 6), ("over_core", 4), ("over_core", 5),
-    ("hidden", 7), ("down", 6), ("over_core", 6), ("partner", 0), ("down_a", 7), ("down_b", 7), ("over_core_a", 7),
+    ("send_far", 0), ("gate_up", 0), ("relay_a", 0), ("forward", 1), ("forward", 2), ("relay_b", 0), ("near_sums", 0),
+    ("gate_up", 1), ("near_sums", 1), ("gate_up", 2), ("forward", 4), ("relay", 1), ("over_y", 0), ("near_sums", 2),
+    ("hidden", 0), ("forward", 3), ("relay", 2), ("gate_up", 3), ("near_sums", 3), ("over_y", 1), ("near", 0),
+    ("over_y", 2), ("send_near", 0), ("relay", 3), ("gate_up", 4), ("far", 0), ("near_sums", 4), ("hidden", 2),
+    ("forward", 5), ("over_y", 3), ("relay", 4), ("hidden", 1), ("forward", 6), ("gate_up", 5), ("near", 2),
+    ("over_y", 4), ("near", 1), ("near_sums", 5), ("down", 0), ("relay", 5), ("far", 1), ("hidden", 3), ("far", 2),
+    ("gate_up", 6), ("hidden", 4), ("over_y", 5), ("near", 3), ("forward", 7), ("over_core", 0), ("relay_a", 6),
+    ("down", 1), ("near", 4), ("far", 3), ("near_sums", 6), ("hidden", 5), ("gate_up", 7), ("over_core", 1),
+    ("far", 4), ("over_y_a", 6), ("down", 2), ("near", 5), ("relay_b", 6), ("down", 3), ("relay_a", 7), ("far", 5),
+    ("near_sums", 7), ("over_y_b", 6), ("over_core", 2), ("relay_b", 7), ("over_core", 3), ("hidden_a", 6),
+    ("down", 4), ("over_y_a", 7), ("down", 5), ("over_y_b", 7), ("hidden_b", 6), ("over_core", 4), ("over_core", 5),
+    ("hidden_a", 7), ("down_first", 6), ("hidden_b", 7), ("down_a", 6), ("down_b", 6), ("over_core_a", 6),
+    ("down_first", 7), ("partner", 0), ("down_a", 7), ("over_core_b", 6), ("down_b", 7), ("over_core_a", 7),
     ("over_core_b", 7),
 )
 
 ALONG_X = {"x2": (2,), "zx1": (1,), "zx2": (2,), "zx3": (3,), "mixA": (1, 3), "mixB": (1, 3)}
-PIECES = ((0, 0, 1024, 0), (0, 1024, 640, 1024), (1, 0, 384, 1664), (1, 384, 1024, 2048), (1, 1408, 256, 3072))
-W_FOR_TILE = ((0,), (1, 2), (3,), (4,))
-NSEM = 176
+PIECES = ((0, 0, 896, 0), (1, 0, 896, 896), (0, 896, 768, 1792), (1, 896, 768, 2560))
+W_FOR_TILE = ((0, 1), (2,), (3,), ())
+GROUPS = ((0, 0, 896), (1792, 896, 768))
+NSEM = 208
+
+
+def sum_columns(g):
+    return pl.ds(0, N2) if g is None else pl.ds(GROUPS[g][0], 2 * GROUPS[g][2])
+
+
+def hidden_columns(g):
+    return pl.ds(0, N) if g is None else pl.ds(GROUPS[g][1], GROUPS[g][2])
+
+
+def parts(c, chunks):
+    return (0, 1) if c in chunks else (None,)
 
 
 def encode(v):
@@ -50,7 +67,7 @@
     return (s * jnp.abs(s)).astype(BF)
 
 
-def body(tok, wg, wu, gs, us, wd, ds, out, W, WD, T, PT, RL, RM, RP, ZR, H, D, CR, XS, XR, ACC, ZLB, ZLR, ssem, rsem, lsem):
+def body(tok, wg, wu, gs_in, us_in, wd, ds_in, out, gs, us, ds, W, WD, T, PT, RL, RM, RP, ZR, H, D, CR, XS, XR, ACC, ZLB, ZLR, ssem, rsem, lsem):
     gx, gy = lax.axis_index("gx"), lax.axis_index("gy")
     zh, y = gx // 4, lax.rem(gx, 4)
     zl, x, core = gy // 8, lax.rem(gy // 2, 4), lax.rem(gy, 2)
@@ -89,8 +106,11 @@
     ]
     own_copy = pltpu.make_async_copy(tok, T.at[CHUNKS.index("own"), core], lsem.at[5])
     wd_copy = pltpu.make_async_copy(wd, WD, lsem.at[6])
+    scale_copies = [
+        pltpu.make_async_copy(a, b, lsem.at[7 + i]) for i, (a, b) in enumerate(((gs_in, gs), (us_in, us), (ds_in, ds)))
+    ]
     own_copy.start()
-    for c in w_copies:
+    for c in w_copies + scale_copies:
         c.start()
 
     barrier = pltpu.get_barrier_semaphore()
@@ -134,50 +154,68 @@
             part = jnp.dot(rows, W[:, pl.ds(n0, width)], preferred_element_type=F32)
             PT[c, :, :, pl.ds(n0, width)] = encode(part).reshape(8, 16, width)
 
-        def step(n, carry):
-            if c == 0:
-                for t in range(3):
-
-                    @pl.when(n == t)
-                    def _():
-                        for i in W_FOR_TILE[t]:
-                            w_copies[i].wait()
-
-            tile(pl.multiple_of(n * 1024, 1024), 1024)
-            return carry
-
-        lax.fori_loop(0, 3, step, 0)
+        def far_sums(g):
+            cols = sum_columns(g)
+            send(PT.at[c, own(y2, 0), :, cols], RL.at[c, 0, :, cols], ("far+", c, g), to_yp)
+            send(PT.at[c, own(y2, 1), :, cols], RL.at[c, 1, :, cols], ("far-", c, g), to_ym)
+
         if c == 0:
-            w_copies[4].wait()
+            for t in range(2):
+                for i in W_FOR_TILE[t]:
+                    w_copies[i].wait()
+                tile(1024 * t, 1024)
+            if c in RS_GROUPS:
+                far_sums(0)
+            w_copies[3].wait()
+            tile(2048, 1024)
+        else:
+
+            def step(n, carry):
+                tile(pl.multiple_of(n * 1024, 1024), 1024)
+                return carry
+
+            lax.fori_loop(0, 3, step, 0)
         tile(3072, 256)
-        send(PT.at[c, own(y2, 0)], RL.at[c, 0], ("far+", c), to_yp)
-        send(PT.at[c, own(y2, 1)], RL.at[c, 1], ("far-", c), to_ym)
-        send(PT.at[c, own(yp, 1)], RM.at[c, 1], ("near+", c), to_yp)
-        send(PT.at[c, own(ym, 0)], RP.at[c, 0], ("near-", c), to_ym)
+        for g in parts(c, RS_GROUPS):
+            if c or g != 0:
+                far_sums(g)
         if c == 0:
             wd_copy.start()
 
-    def relay(c):
-        arrived(RL.at[c, 0], ("far+", c))
-        o = own(yp, 0)
-        PT[c, o] = recode(decode(PT[c, o]) + decode(RL[c, 0]))
-        send(PT.at[c, o], RM.at[c, 0], ("via+", c), to_yp)
-        arrived(RL.at[c, 1], ("far-", c))
-        o = own(ym, 1)
-        PT[c, o] = recode(decode(PT[c, o]) + decode(RL[c, 1]))
-        send(PT.at[c, o], RP.at[c, 1], ("via-", c), to_ym)
-
-    def over_y(c):
-        arrived(RM.at[c, 1], ("near+", c))
-        arrived(RP.at[c, 0], ("near-", c))
-        arrived(RM.at[c, 0], ("via+", c))
-        arrived(RP.at[c, 1], ("via-", c))
-        o = own(y, zo)
-        PT[c, o] = recode(decode(PT[c, o]) + decode(RM[c, zo]) + decode(RP[c, zo]))
-        send(PT.at[c, o], ZR.at[c], ("z_hi", c), to_zh)
-
-    def hidden(c):
-        arrived(ZR.at[c], ("z_hi", c))
+    def near_sums(c):
+        if c == 0:
+            for scale in scale_copies:
+                scale.wait()
+        for g in parts(c, RS_GROUPS):
+            cols = sum_columns(g)
+            send(PT.at[c, own(yp, 1), :, cols], RM.at[c, 1, :, cols], ("near+", c, g), to_yp)
+            send(PT.at[c, own(ym, 0), :, cols], RP.at[c, 0, :, cols], ("near-", c, g), to_ym)
+
+    def relay(c, g=None):
+        cols = sum_columns(g)
+        for i, (o, dst, far, via, to) in enumerate(
+            ((own(yp, 0), RM, "far+", "via+", to_yp), (own(ym, 1), RP, "far-", "via-", to_ym))
+        ):
+            arrived(RL.at[c, i, :, cols], (far, c, g))
+            PT[c, o, :, cols] = recode(decode(PT[c, o, :, cols]) + decode(RL[c, i, :, cols]))
+            send(PT.at[c, o, :, cols], dst.at[c, i, :, cols], (via, c, g), to)
+
+    def over_y(c, g=None):
+        for h in parts(c, RS_GROUPS):
+            if g is None or g == h:
+                cols = sum_columns(h)
+                arrived(RM.at[c, 1, :, cols], ("near+", c, h))
+                arrived(RP.at[c, 0, :, cols], ("near-", c, h))
+                arrived(RM.at[c, 0, :, cols], ("via+", c, h))
+                arrived(RP.at[c, 1, :, cols], ("via-", c, h))
+        o, cols = own(y, zo), sum_columns(g)
+        PT[c, o, :, cols] = recode(
+            decode(PT[c, o, :, cols]) + decode(RM[c, zo, :, cols]) + decode(RP[c, zo, :, cols])
+        )
+        send(PT.at[c, o, :, cols], ZR.at[c, :, cols], ("z_hi", c, g), to_zh)
+
+    def hidden(c, g=None):
+        arrived(ZR.at[c, :, sum_columns(g)], ("z_hi", c, g))
         o = own(y, zh)
 
         def total(cols):
@@ -186,58 +224,62 @@
                 + decode(RP[c, zh, :, cols]) + decode(ZR[c, :, cols])
             )
 
-        gate = total(pl.ds(0, N)) * (gs[...] * (1.0 / LIFT))[None, :]
-        up = total(pl.ds(N, N)) * (us[...] * (1.0 / LIFT))[None, :]
-        H[c, o] = (jax.nn.silu(gate) * up).astype(BF)
-        rows = H.at[c, o]
-        send(rows, rows, ("h+", c), to_yp)
-        send(rows, rows, ("h-", c), to_ym)
-        send(rows, rows, ("hz", c), to_zh)
+        for h in (0, 1):
+            if g is None or g == h:
+                first, _, width = GROUPS[h]
+                units = hidden_columns(h)
+                gate = total(pl.ds(first, width)) * (gs[units] * (1.0 / LIFT))[None, :]
+                up = total(pl.ds(first + width, width)) * (us[units] * (1.0 / LIFT))[None, :]
+                H[c, o, :, units] = (jax.nn.silu(gate) * up).astype(BF)
+        rows = H.at[c, o, :, hidden_columns(g)]
+        send(rows, rows, ("h+", c, g), to_yp)
+        send(rows, rows, ("h-", c, g), to_ym)
+        send(rows, rows, ("hz", c, g), to_zh)
         if c in DIRECT:
-            send(rows, rows, ("hz+", c), to_zh_yp)
-            send(rows, rows, ("hz-", c), to_zh_ym)
-            send(rows, rows, ("h2", c), to_y2)
-            send(rows, rows, ("hz2", c), to_zh_y2)
+            send(rows, rows, ("hz+", c, g), to_zh_yp)
+            send(rows, rows, ("hz-", c, g), to_zh_ym)
+            send(rows, rows, ("h2", c, g), to_y2)
+            send(rows, rows, ("hz2", c, g), to_zh_y2)
 
     def near(c):
         rows = H.at[c, own(ym, zh)]
-        arrived(rows, ("h+", c))
+        arrived(rows, ("h+", c, None))
         left = rows.at[:, pl.ds(0, HALF)]
         send(left, left, ("hv+", c), to_yp)
-        send(rows, rows, ("hz+", c), to_zh)
+        send(rows, rows, ("hz+", c, None), to_zh)
         rows = H.at[c, own(yp, zh)]
-        arrived(rows, ("h-", c))
+        arrived(rows, ("h-", c, None))
         right = rows.at[:, pl.ds(HALF, N - HALF)]
         send(right, right, ("hv-", c), to_ym)
-        send(rows, rows, ("hz-", c), to_zh)
+        send(rows, rows, ("hz-", c, None), to_zh)
 
     def far(c):
         rows = H.at[c, own(y2, zh)]
         arrived(rows.at[:, pl.ds(0, HALF)], ("hv+", c))
         arrived(rows.at[:, pl.ds(HALF, N - HALF)], ("hv-", c))
-        send(rows, rows, ("hz2", c), to_zh)
+        send(rows, rows, ("hz2", c, None), to_zh)
 
     def down_tile(c, n):
-        cols = pl.ds(n * 1024, 1024) if isinstance(n, int) else pl.ds(pl.multiple_of(n * 1024, 1024), 1024)
+        cols = pl.ds(pl.multiple_of(n * 1024, 1024), 1024)
         rows = H[c].reshape(128, N)
         part = jnp.dot(rows, WD[:, cols], preferred_element_type=F32)
         D[c % 2, :, :, cols] = part.reshape(2, 64, 1024)
 
+    def hidden_arrived(c, g):
+        keys = [("hz", y, zo), ("hz+", ym, zo), ("hz-", yp, zo), ("hz2", y2, zo)]
+        if c in DIRECT:
+            keys += [("h+", ym, zh), ("h-", yp, zh), ("h2", y2, zh)]
+        for key, y_, z_ in keys:
+            arrived(H.at[c, own(y_, z_), :, hidden_columns(g)], (key, c, g))
+
     def before_down(c):
-        if c in DIRECT:
-            arrived(H.at[c, own(ym, zh)], ("h+", c))
-            arrived(H.at[c, own(yp, zh)], ("h-", c))
-            arrived(H.at[c, own(y2, zh)], ("h2", c))
-        arrived(H.at[c, own(y, zo)], ("hz", c))
-        arrived(H.at[c, own(ym, zo)], ("hz+", c))
-        arrived(H.at[c, own(yp, zo)], ("hz-", c))
-        arrived(H.at[c, own(y2, zo)], ("hz2", c))
         if c == 0:
             wd_copy.wait()
         if c >= 2:
             on_way.pop(("core", c - 2)).wait_send()
 
     def down(c):
+        hidden_arrived(c, None)
         before_down(c)
 
         def step(n, carry):
@@ -247,11 +289,26 @@
         lax.fori_loop(0, 2, step, 0)
         send(D.at[c % 2, other], CR.at[c], ("core", c), to_core)
 
-    def down_part(c, n):
+    def down_first(c):
+        hidden_arrived(c, 0)
+        before_down(c)
+
+        def step(n, carry):
+            cols = pl.ds(pl.multiple_of(n * 1024, 1024), 1024)
+            rows = H[c, :, :, pl.ds(0, 896)].reshape(128, 896)
+            part = jnp.dot(rows, WD[pl.ds(0, 896), cols], preferred_element_type=F32)
+            D[c % 2, :, :, cols] = part.reshape(2, 64, 1024)
+            return carry
+
+        lax.fori_loop(0, 2, step, 0)
+
+    def down_rest(c, n):
         if n == 0:
-            before_down(c)
-        down_tile(c, n)
+            hidden_arrived(c, 1)
         cols = pl.ds(n * 1024, 1024)
+        rows = H[c, :, :, pl.ds(896, 768)].reshape(128, 768)
+        part = jnp.dot(rows, WD[pl.ds(896, 768), cols], preferred_element_type=F32)
+        D[c % 2, :, :, cols] += part.reshape(2, 64, 1024)
         send(D.at[c % 2, other, :, cols], CR.at[c, :, cols], ("core", c, n), to_core)
 
     def add_cores(c, cols, tag):
@@ -297,14 +354,21 @@
     send(tok, T.at[CHUNKS.index("z"), core], z_key, to_zl)
 
     steps = dict(
-        send_far=send_far, send_near=send_near, forward=forward, gate_up=gate_up, relay=relay, over_y=over_y,
+        send_far=send_far, send_near=send_near, forward=forward, gate_up=gate_up, near_sums=near_sums, relay=relay, over_y=over_y,
         hidden=hidden, near=near, far=far, down=down, over_core=over_core, partner=partner,
-        down_a=lambda c: down_part(c, 0), down_b=lambda c: down_part(c, 1),
+        relay_a=lambda c: relay(c, 0), relay_b=lambda c: relay(c, 1),
+        over_y_a=lambda c: over_y(c, 0), over_y_b=lambda c: over_y(c, 1),
+        hidden_a=lambda c: hidden(c, 0), hidden_b=lambda c: hidden(c, 1),
+        down_first=down_first, down_a=lambda c: down_rest(c, 0), down_b=lambda c: down_rest(c, 1),
         over_core_a=lambda c: add_cores(c, pl.ds(0, 1024), (0,)),
         over_core_b=lambda c: add_cores(c, pl.ds(1024, 1024), (1,)),
     )
     for name, c in ORDER:
         steps[name](c)
+
+    for key in list(on_way):
+        if key[0] not in ("x", "z_lo", "core") or (key[0] == "x" and key[1] not in SPLIT):
+            on_way.pop(key).wait_send()
 
     c2, ca, cb = CHUNKS.index("x2"), CHUNKS.index("mixA"), CHUNKS.index("mixB")
     sums_arrived(c2)
@@ -327,9 +391,12 @@
         body,
         name="gated_layer",
         out_shape=jax.ShapeDtypeStruct((64, M), BF),
-        in_specs=[hbm, hbm, hbm, vmem, vmem, hbm, vmem],
+        in_specs=[hbm] * 7,
         out_specs=vmem,
         scratch_shapes=[
+            pltpu.VMEM((N,), F32),
+            pltpu.VMEM((N,), F32),
+            pltpu.VMEM((M,), F32),
             pltpu.VMEM((K, N2), BF),
             pltpu.VMEM((N, M), BF),
             pltpu.VMEM((NC, 2, 64, K), BF),
@@ -348,7 +415,7 @@
             pltpu.VMEM((64, M), BF),
             pltpu.SemaphoreType.DMA((NSEM,)),
             pltpu.SemaphoreType.DMA((NSEM,)),
-            pltpu.SemaphoreType.DMA((7,)),
+            pltpu.SemaphoreType.DMA((10,)),
         ],
         compiler_params=pltpu.CompilerParams(
             collective_id=0, has_side_effects=True, vmem_limit_bytes=62 * 2**20

time: 111 us -> 108 us (0.973)
  Pallas kernels: 110 us -> 106 us
    pallas_call x1, Pallas kernels: 110 us -> 106 us  [on_device(): pl.pallas_call(body, name='gated_layer', out_shape=jax.ShapeDtypeStruct((...]
where the time goes in v3:
time: 108 us
  Pallas kernels  106 us (98%)
  local copies, waits for them, and re-layouts  1.67 us (2%)
    pallas_call x1, Pallas kernels, on_device(): pl.pallas_call(body, name='gated_layer', out_shape=jax.ShapeDtypeStruct((...  106 us

profile of v3, /device:TPU:1, one launch (start us, length us, event | category | flops | bytes accessed | tf_op | source)
XLA Modules:
  0.0 107.7 jit_solution(17073672113070944389)
XLA Ops:
  0.0 106.0 %gated_layer.1 = bf16[64,2048]{1,0:T(8,128)(2,1)} custom-call(bf16[64,2048]{1,0:T(8,128)(2,1)} %tok.1, bf16[2048,1664]{1,0:T(8,128)(2,1)} %wg.1, bf16[2048,1664]{1,0:T(8,128)(2,1)} %wu.1, f32[1664]{0:T(1024)} %gs_in.1, f32[1664]{0:T(1024)} %us_in.1, bf16[1664,2048]{1,0:T(8,128)(2,1)} %wd.1, f32[2048]{0:T(1024)} %ds_in.1), custom_call_target="tpu_custom_call" | custom-call | flops 20937965568 | bytes 20447232 | tf_op jit(solution)/shard_map/gated_layer/pallas_call | solution.py:390
  106.0 1.7 %copy.9 = bf16[64,2048]{1,0:T(8,128)(2,1)} copy(bf16[64,2048]{1,0:T(8,128)(2,1)} %gated_layer.1) | data formatting | bytes 524288

commit v4 on v3

--- a/solution.py
+++ b/solution.py
@@ -13,28 +13,30 @@
 LIFT = 2.0**50
 TINY = 1e-37
 
-CHUNKS = ("own", "x2", "z", "zx2", "zx1", "zx3", "mixA", "mixB")
-DIRECT = (6, 7)
+CHUNKS = ("own", "z", "x2", "zx2", "zmixA", "zmixB", "mixA", "mixB")
+DIRECT = (7,)
+Z_SUMS_FIRST = (3,)
+Z_FIRST = (6,)
 SPLIT = (6, 7)
 RS_GROUPS = (0, 6, 7)
 ORDER = (
-    ("send_far", 0), ("gate_up", 0), ("relay_a", 0), ("forward", 1), ("forward", 2), ("relay_b", 0), ("near_sums", 0),
-    ("gate_up", 1), ("near_sums", 1), ("gate_up", 2), ("forward", 4), ("relay", 1), ("over_y", 0), ("near_sums", 2),
-    ("hidden", 0), ("forward", 3), ("relay", 2), ("gate_up", 3), ("near_sums", 3), ("over_y", 1), ("near", 0),
-    ("over_y", 2), ("send_near", 0), ("relay", 3), ("gate_up", 4), ("far", 0), ("near_sums", 4), ("hidden", 2),
-    ("forward", 5), ("over_y", 3), ("relay", 4), ("hidden", 1), ("forward", 6), ("gate_up", 5), ("near", 2),
-    ("over_y", 4), ("near", 1), ("near_sums", 5), ("down", 0), ("relay", 5), ("far", 1), ("hidden", 3), ("far", 2),
-    ("gate_up", 6), ("hidden", 4), ("over_y", 5), ("near", 3), ("forward", 7), ("over_core", 0), ("relay_a", 6),
-    ("down", 1), ("near", 4), ("far", 3), ("near_sums", 6), ("hidden", 5), ("gate_up", 7), ("over_core", 1),
-    ("far", 4), ("over_y_a", 6), ("down", 2), ("near", 5), ("relay_b", 6), ("down", 3), ("relay_a", 7), ("far", 5),
-    ("near_sums", 7), ("over_y_b", 6), ("over_core", 2), ("relay_b", 7), ("over_core", 3), ("hidden_a", 6),
-    ("down", 4), ("over_y_a", 7), ("down", 5), ("over_y_b", 7), ("hidden_b", 6), ("over_core", 4), ("over_core", 5),
-    ("hidden_a", 7), ("down_first", 6), ("hidden_b", 7), ("down_a", 6), ("down_b", 6), ("over_core_a", 6),
-    ("down_first", 7), ("partner", 0), ("down_a", 7), ("over_core_b", 6), ("down_b", 7), ("over_core_a", 7),
-    ("over_core_b", 7),
+    ("send_far", 0), ("gate_up", 0), ("near_sums", 0), ("forward", 1), ("relay_a", 0), ("relay_b", 0), ("forward", 2),
+    ("gate_up", 1), ("near_sums", 1), ("over_y", 0), ("gate_up", 2), ("forward", 3), ("hidden", 0), ("near_sums", 2),
+    ("gate_up", 3), ("send_near", 0), ("relay", 1), ("forward", 4), ("forward", 5), ("relay", 2), ("gate_up", 4),
+    ("gate_up", 5), ("near_sums", 4), ("over_y", 1), ("over_y", 2), ("near", 0), ("relay", 4), ("near_sums", 3),
+    ("forward", 6), ("far", 0), ("hidden", 2), ("over_y", 4), ("forward", 7), ("hidden", 1), ("relay", 3),
+    ("near_sums", 5), ("down", 0), ("near", 2), ("near", 1), ("relay", 5), ("hidden", 3), ("gate_up", 6),
+    ("over_core", 0), ("far", 1), ("far", 2), ("hidden", 4), ("over_y", 5), ("near", 3), ("relay_a", 6), ("down", 1),
+    ("relay_b", 6), ("near", 4), ("near_sums", 6), ("gate_up", 7), ("far", 3), ("down", 2), ("over_core", 1),
+    ("far", 4), ("over_y_a", 6), ("hidden", 5), ("near_sums", 7), ("over_y_b", 6), ("relay_a", 7), ("over_core", 2),
+    ("down", 3), ("near", 5), ("down", 4), ("hidden_a", 6), ("relay_b", 7), ("hidden_b", 6), ("over_core", 3),
+    ("over_y_a", 7), ("far", 5), ("pass_on_a", 6), ("over_core", 4), ("over_y_b", 7), ("pass_on_b", 6),
+    ("hidden_a", 7), ("down", 5), ("hidden_b", 7), ("down_first", 6), ("down_a", 6), ("down_b", 6), ("over_core", 5),
+    ("partner_a", 0), ("over_core_a", 6), ("down_first", 7), ("down_a", 7), ("down_b", 7), ("over_core_b", 6),
+    ("over_core_a", 7), ("partner_b", 0), ("over_core_b", 7),
 )
 
-ALONG_X = {"x2": (2,), "zx1": (1,), "zx2": (2,), "zx3": (3,), "mixA": (1, 3), "mixB": (1, 3)}
+ALONG_X = {"x2": (2,), "zx1": (1,), "zx2": (2,), "zx3": (3,), "mixA": (1, 3), "mixB": (1, 3), "zmixA": (1, 3), "zmixB": (1, 3)}
 PIECES = ((0, 0, 896, 0), (1, 0, 896, 896), (0, 896, 768, 1792), (1, 896, 768, 2560))
 W_FOR_TILE = ((0, 1), (2,), (3,), ())
 GROUPS = ((0, 0, 896), (1792, 896, 768))
@@ -67,7 +69,7 @@
     return (s * jnp.abs(s)).astype(BF)
 
 
-def body(tok, wg, wu, gs_in, us_in, wd, ds_in, out, gs, us, ds, W, WD, T, PT, RL, RM, RP, ZR, H, D, CR, XS, XR, ACC, ZLB, ZLR, ssem, rsem, lsem):
+def body(tok, wg, wu, gs_in, us_in, wd, ds_in, out, gs, us, ds, W, WD, T, PT, RL, RM, RP, ZX, ZR, H, D, CR, XS, XR, ACC, ZLB, ZLR, ssem, rsem, lsem):
     gx, gy = lax.axis_index("gx"), lax.axis_index("gy")
     zh, y = gx // 4, lax.rem(gx, 4)
     zl, x, core = gy // 8, lax.rem(gy // 2, 4), lax.rem(gy, 2)
@@ -121,28 +123,33 @@
 
     def chunk_tokens(c):
         name = CHUNKS[c]
-        if name[:3] == "mix":
+        if "mix" in name:
             return [(T.at[c, core, pl.ds(32 * i, 32)], ("tok", name, d)) for i, d in enumerate((1, 3))]
         return [(T.at[c, core], ("tok", name))]
 
     def send_far(_):
         send(tok, T.at[CHUNKS.index("x2"), core], ("tok", "x2"), to_x[2])
 
+    def mixed(rows, name):
+        c = CHUNKS.index(name)
+        rows = rows.at[pl.ds(32 * "AB".index(name[-1]), 32)]
+        send(rows, T.at[c, core, pl.ds(32, 32)], ("tok", name, 3), to_x[1])
+        send(rows, T.at[c, core, pl.ds(0, 32)], ("tok", name, 1), to_x[3])
+
     def send_near(_):
-        for i, name in enumerate(("mixA", "mixB")):
-            c = CHUNKS.index(name)
-            rows = tok.at[pl.ds(32 * i, 32)]
-            send(rows, T.at[c, core, pl.ds(32, 32)], ("tok", name, 3), to_x[1])
-            send(rows, T.at[c, core, pl.ds(0, 32)], ("tok", name, 1), to_x[3])
+        mixed(tok, "mixA")
+        mixed(tok, "mixB")
 
     def forward(c):
         for where, key in chunk_tokens(c):
             arrived(where, key)
         send(T.at[c, core], T.at[c, core], ("fwd", c), to_core)
         if CHUNKS[c] == "z":
-            for d in (1, 3, 2):
-                name = "zx%d" % (4 - d)
-                send(T.at[c, core], T.at[CHUNKS.index(name), core], ("tok", name), to_x[d])
+            for name in CHUNKS:
+                if name[:2] == "zx":
+                    send(T.at[c, core], T.at[CHUNKS.index(name), core], ("tok", name), to_x[4 - int(name[2])])
+                if name[:4] == "zmix":
+                    mixed(T.at[c, core], name)
 
     def gate_up(c):
         if CHUNKS[c] == "own":
@@ -176,13 +183,46 @@
 
             lax.fori_loop(0, 3, step, 0)
         tile(3072, 256)
-        for g in parts(c, RS_GROUPS):
-            if c or g != 0:
-                far_sums(g)
+        if c in Z_SUMS_FIRST:
+            for j in range(4):
+                send(PT.at[c, own(j, zo)], ZX.at[j], ("z_first", c, j), to_zh)
+        else:
+            for g in parts(c, RS_GROUPS):
+                if c or g != 0:
+                    far_sums(g)
         if c == 0:
             wd_copy.start()
 
+    def z_sums(c):
+        for j in range(4):
+            arrived(ZX.at[j], ("z_first", c, j))
+        a, b = sum_columns(0), sum_columns(1)
+
+        def add(y_):
+            o = own(y_, zh)
+            PT[c, o] = recode(decode(PT[c, o]) + decode(ZX[y_]))
+            return PT.at[c, o]
+
+        far = add(y2)
+        send(far.at[:, a], RL.at[c, 0, :, a], ("far+", c), to_yp)
+        send(far.at[:, b], RL.at[c, 1, :, b], ("far-", c), to_ym)
+        send(add(yp).at[:, b], RM.at[c, 0, :, b], ("near+", c), to_yp)
+        send(add(ym).at[:, a], RP.at[c, 0, :, a], ("near-", c), to_ym)
+        add(y)
+
+    def relay_z_sums(c):
+        for i, (y_, g, dst, far, via, to) in enumerate(
+            ((yp, 0, RM, "far+", "via+", to_yp), (ym, 1, RP, "far-", "via-", to_ym))
+        ):
+            o, cols = own(y_, zh), sum_columns(g)
+            arrived(RL.at[c, i, :, cols], (far, c))
+            PT[c, o, :, cols] = recode(decode(PT[c, o, :, cols]) + decode(RL[c, i, :, cols]))
+            send(PT.at[c, o, :, cols], dst.at[c, 0, :, cols], (via, c), to)
+
     def near_sums(c):
+        if c in Z_SUMS_FIRST:
+            z_sums(c)
+            return
         if c == 0:
             for scale in scale_copies:
                 scale.wait()
@@ -192,6 +232,9 @@
             send(PT.at[c, own(ym, 0), :, cols], RP.at[c, 0, :, cols], ("near-", c, g), to_ym)
 
     def relay(c, g=None):
+        if c in Z_SUMS_FIRST:
+            relay_z_sums(c)
+            return
         cols = sum_columns(g)
         for i, (o, dst, far, via, to) in enumerate(
             ((own(yp, 0), RM, "far+", "via+", to_yp), (own(ym, 1), RP, "far-", "via-", to_ym))
@@ -215,10 +258,17 @@
         send(PT.at[c, o, :, cols], ZR.at[c, :, cols], ("z_hi", c, g), to_zh)
 
     def hidden(c, g=None):
-        arrived(ZR.at[c, :, sum_columns(g)], ("z_hi", c, g))
         o = own(y, zh)
+        if c in Z_SUMS_FIRST:
+            for h, plus, minus in ((0, "via+", "near-"), (1, "near+", "via-")):
+                arrived(RM.at[c, 0, :, sum_columns(h)], (plus, c))
+                arrived(RP.at[c, 0, :, sum_columns(h)], (minus, c))
+        else:
+            arrived(ZR.at[c, :, sum_columns(g)], ("z_hi", c, g))
 
         def total(cols):
+            if c in Z_SUMS_FIRST:
+                return decode(PT[c, o, :, cols]) + decode(RM[c, 0, :, cols]) + decode(RP[c, 0, :, cols])
             return (
                 decode(PT[c, o, :, cols]) + decode(RM[c, zh, :, cols])
                 + decode(RP[c, zh, :, cols]) + decode(ZR[c, :, cols])
@@ -235,11 +285,19 @@
         send(rows, rows, ("h+", c, g), to_yp)
         send(rows, rows, ("h-", c, g), to_ym)
         send(rows, rows, ("hz", c, g), to_zh)
+        if c in DIRECT + Z_FIRST:
+            send(rows, rows, ("h2", c, g), to_y2)
         if c in DIRECT:
             send(rows, rows, ("hz+", c, g), to_zh_yp)
             send(rows, rows, ("hz-", c, g), to_zh_ym)
-            send(rows, rows, ("h2", c, g), to_y2)
             send(rows, rows, ("hz2", c, g), to_zh_y2)
+
+    def pass_on(c, g=None):
+        rows = H.at[c, own(y, zo), :, hidden_columns(g)]
+        arrived(rows, ("hz", c, g))
+        send(rows, rows, ("hz+", c, g), to_yp)
+        send(rows, rows, ("hz-", c, g), to_ym)
+        send(rows, rows, ("hz2", c, g), to_y2)
 
     def near(c):
         rows = H.at[c, own(ym, zh)]
@@ -267,7 +325,9 @@
 
     def hidden_arrived(c, g):
         keys = [("hz", y, zo), ("hz+", ym, zo), ("hz-", yp, zo), ("hz2", y2, zo)]
-        if c in DIRECT:
+        if c in Z_FIRST:
+            keys = keys[1:]
+        if c in DIRECT + Z_FIRST:
             keys += [("h+", ym, zh), ("h-", yp, zh), ("h2", y2, zh)]
         for key, y_, z_ in keys:
             arrived(H.at[c, own(y_, z_), :, hidden_columns(g)], (key, c, g))
@@ -340,14 +400,17 @@
             else:
                 arrived(XR.at[c, part], ("x", c, i))
 
-    def partner(_):
-        total = ACC[1]
-        for name in ("zx1", "zx2", "zx3"):
-            c = CHUNKS.index(name)
-            sums_arrived(c)
-            total = total + XR[c].astype(F32)
-        ZLB[...] = total.astype(BF)
-        send(ZLB, ZLR, ("z_lo",), to_zl)
+    def partner(i):
+        whole = CHUNKS.index("zx2")
+        half = CHUNKS.index(("zmixA", "zmixB")[i])
+        if i == 0:
+            sums_arrived(whole)
+        sums_arrived(half)
+        rows = pl.ds(32 * i, 32)
+        total = ACC[1, rows] + XR[whole, rows].astype(F32)
+        total = total + XR[half, 0:32].astype(F32) + XR[half, 32:64].astype(F32)
+        ZLB[rows] = total.astype(BF)
+        send(ZLB.at[rows], ZLR.at[rows], ("z_lo", i), to_zl)
 
     own_key, z_key = ("fwd", CHUNKS.index("own")), ("tok", "z")
     send(tok, T.at[CHUNKS.index("own"), core], own_key, to_core)
@@ -355,10 +418,11 @@
 
     steps = dict(
         send_far=send_far, send_near=send_near, forward=forward, gate_up=gate_up, near_sums=near_sums, relay=relay, over_y=over_y,
-        hidden=hidden, near=near, far=far, down=down, over_core=over_core, partner=partner,
+        hidden=hidden, near=near, far=far, down=down, over_core=over_core, partner_a=lambda _: partner(0), partner_b=lambda _: partner(1),
         relay_a=lambda c: relay(c, 0), relay_b=lambda c: relay(c, 1),
         over_y_a=lambda c: over_y(c, 0), over_y_b=lambda c: over_y(c, 1),
         hidden_a=lambda c: hidden(c, 0), hidden_b=lambda c: hidden(c, 1),
+        pass_on=pass_on, pass_on_a=lambda c: pass_on(c, 0), pass_on_b=lambda c: pass_on(c, 1),
         down_first=down_first, down_a=lambda c: down_rest(c, 0), down_b=lambda c: down_rest(c, 1),
         over_core_a=lambda c: add_cores(c, pl.ds(0, 1024), (0,)),
         over_core_b=lambda c: add_cores(c, pl.ds(1024, 1024), (1,)),
@@ -372,13 +436,12 @@
 
     c2, ca, cb = CHUNKS.index("x2"), CHUNKS.index("mixA"), CHUNKS.index("mixB")
     sums_arrived(c2)
-    base = ACC[0] + XR[c2].astype(F32)
-    arrived(ZLR, ("z_lo",))
-    base = base + ZLR[...].astype(F32)
     for i, c in enumerate((ca, cb)):
+        rows = pl.ds(32 * i, 32)
+        arrived(ZLR.at[rows], ("z_lo", i))
+        total = ACC[0, rows] + XR[c2, rows].astype(F32) + ZLR[rows].astype(F32)
         sums_arrived(c)
-        rows = slice(32 * i, 32 * i + 32)
-        total = base[rows] + XR[c, 0:32].astype(F32) + XR[c, 32:64].astype(F32)
+        total = total + XR[c, 0:32].astype(F32) + XR[c, 32:64].astype(F32)
         out[rows, :] = (total * ds[...][None, :]).astype(BF)
 
     for c in on_way.values():
@@ -390,7 +453,7 @@
     return pl.pallas_call(
         body,
         name="gated_layer",
-        out_shape=jax.ShapeDtypeStruct((64, M), BF),
+        out_shape=pltpu.VMEM((64, M), BF),
         in_specs=[hbm] * 7,
         out_specs=vmem,
         scratch_shapes=[
@@ -404,6 +467,7 @@
             pltpu.VMEM((NC, 2, 16, N2), BF),
             pltpu.VMEM((NC, 2, 16, N2), BF),
             pltpu.VMEM((NC, 2, 16, N2), BF),
+            pltpu.VMEM((4, 16, N2), BF),
             pltpu.VMEM((NC, 16, N2), BF),
             pltpu.VMEM((NC, 8, 16, N), BF),
             pltpu.VMEM((2, 2, 64, M), F32),

time: 108 us -> 101 us (0.935)
  Pallas kernels: 106 us -> 100 us
    pallas_call x1, Pallas kernels: 106 us -> 100 us  [on_device(): pl.pallas_call(body, name='gated_layer', out_shape=pltpu.VMEM((64, M), BF...]
where the time goes in v4:
time: 101 us
  Pallas kernels  100 us (99%)
    pallas_call x1, Pallas kernels, on_device(): pl.pallas_call(body, name='gated_layer', out_shape=pltpu.VMEM((64, M), BF...  100 us

profile of v4, /device:TPU:1, one launch (start us, length us, event | category | flops | bytes accessed | tf_op | source)
XLA Modules:
  0.0 101.0 jit_solution(3757891545046203658)
XLA Ops:
  0.0 100.3 %gated_layer.1 = bf16[64,2048]{1,0:T(8,128)(2,1)S(1)} custom-call(bf16[64,2048]{1,0:T(8,128)(2,1)} %tok.1, bf16[2048,1664]{1,0:T(8,128)(2,1)} %wg.1, bf16[2048,1664]{1,0:T(8,128)(2,1)} %wu.1, f32[1664]{0:T(1024)} %gs_in.1, f32[1664]{0:T(1024)} %us_in.1, bf16[1664,2048]{1,0:T(8,128)(2,1)} %wd.1, f32[2048]{0:T(1024)} %ds_in.1), custom_call_target="tpu_custom_call" | custom-call | flops 20937965568 | bytes 20447232 | tf_op jit(solution)/shard_map/gated_layer/pallas_call | solution.py:453
  100.3 0.7 copy.9

commit v5 on v4

--- a/solution.py
+++ b/solution.py
@@ -19,21 +19,24 @@
 Z_FIRST = (6,)
 SPLIT = (6, 7)
 RS_GROUPS = (0, 6, 7)
+(
+    FORWARD, GATE_UP, NEAR_SUMS, RELAY, OVER_Y, HIDDEN, NEAR, FAR, DOWN, OVER_CORE, DOWN_A, DOWN_B, DOWN_FIRST,
+    PASS_ON, PASS_ON_A, PASS_ON_B, RELAY_A, RELAY_B, OVER_Y_A, OVER_Y_B, HIDDEN_A, HIDDEN_B, OVER_CORE_A,
+    OVER_CORE_B, PARTNER_A, PARTNER_B, SEND_FAR, SEND_NEAR,
+) = range(28)
 ORDER = (
-    ("send_far", 0), ("gate_up", 0), ("near_sums", 0), ("forward", 1), ("relay_a", 0), ("relay_b", 0), ("forward", 2),
-    ("gate_up", 1), ("near_sums", 1), ("over_y", 0), ("gate_up", 2), ("forward", 3), ("hidden", 0), ("near_sums", 2),
-    ("gate_up", 3), ("send_near", 0), ("relay", 1), ("forward", 4), ("forward", 5), ("relay", 2), ("gate_up", 4),
-    ("gate_up", 5), ("near_sums", 4), ("over_y", 1), ("over_y", 2), ("near", 0), ("relay", 4), ("near_sums", 3),
-    ("forward", 6), ("far", 0), ("hidden", 2), ("over_y", 4), ("forward", 7), ("hidden", 1), ("relay", 3),
-    ("near_sums", 5), ("down", 0), ("near", 2), ("near", 1), ("relay", 5), ("hidden", 3), ("gate_up", 6),
-    ("over_core", 0), ("far", 1), ("far", 2), ("hidden", 4), ("over_y", 5), ("near", 3), ("relay_a", 6), ("down", 1),
-    ("relay_b", 6), ("near", 4), ("near_sums", 6), ("gate_up", 7), ("far", 3), ("down", 2), ("over_core", 1),
-    ("far", 4), ("over_y_a", 6), ("hidden", 5), ("near_sums", 7), ("over_y_b", 6), ("relay_a", 7), ("over_core", 2),
-    ("down", 3), ("near", 5), ("down", 4), ("hidden_a", 6), ("relay_b", 7), ("hidden_b", 6), ("over_core", 3),
-    ("over_y_a", 7), ("far", 5), ("pass_on_a", 6), ("over_core", 4), ("over_y_b", 7), ("pass_on_b", 6),
-    ("hidden_a", 7), ("down", 5), ("hidden_b", 7), ("down_first", 6), ("down_a", 6), ("down_b", 6), ("over_core", 5),
-    ("partner_a", 0), ("over_core_a", 6), ("down_first", 7), ("down_a", 7), ("down_b", 7), ("over_core_b", 6),
-    ("over_core_a", 7), ("partner_b", 0), ("over_core_b", 7),
+    (SEND_FAR, 0), (GATE_UP, 0), (NEAR_SUMS, 0), (FORWARD, 1), (RELAY_A, 0), (FORWARD, 2), (RELAY_B, 0),
+    (GATE_UP, 1), (NEAR_SUMS, 1), (OVER_Y, 0), (GATE_UP, 2), (FORWARD, 3), (SEND_NEAR, 0), (NEAR_SUMS, 2),
+    (HIDDEN, 0), (FORWARD, 4), (GATE_UP, 3), (RELAY, 2), (RELAY, 1), (GATE_UP, 4), (NEAR, 0), (FORWARD, 5),
+    (GATE_UP, 5), (NEAR_SUMS, 4), (FORWARD, 7), (RELAY, 4), (OVER_Y, 1), (OVER_Y, 2), (FAR, 0), (NEAR_SUMS, 3),
+    (HIDDEN, 1), (OVER_Y, 4), (HIDDEN, 2), (RELAY, 3), (FORWARD, 6), (NEAR, 1), (RELAY, 5), (DOWN, 0), (HIDDEN, 4),
+    (HIDDEN, 3), (FAR, 1), (NEAR, 2), (NEAR_SUMS, 5), (GATE_UP, 6), (NEAR, 3), (FAR, 2), (GATE_UP, 7), (OVER_Y, 5),
+    (RELAY_A, 6), (DOWN, 1), (FAR, 3), (NEAR, 4), (NEAR_SUMS, 6), (OVER_CORE, 0), (RELAY_B, 6), (DOWN, 2), (FAR, 4),
+    (HIDDEN, 5), (OVER_CORE, 1), (NEAR_SUMS, 7), (DOWN, 3), (OVER_Y_A, 6), (RELAY_A, 7), (OVER_CORE, 2),
+    (OVER_Y_B, 6), (NEAR, 5), (RELAY_B, 7), (DOWN, 4), (HIDDEN_A, 6), (HIDDEN_B, 6), (OVER_Y_A, 7), (OVER_CORE, 3),
+    (FAR, 5), (OVER_Y_B, 7), (OVER_CORE, 4), (PASS_ON_A, 6), (PASS_ON_B, 6), (HIDDEN_A, 7), (DOWN, 5), (HIDDEN_B, 7),
+    (DOWN_FIRST, 6), (DOWN_A, 6), (OVER_CORE, 5), (PARTNER_A, 0), (OVER_CORE_A, 6), (DOWN_B, 6), (DOWN_FIRST, 7),
+    (DOWN_A, 7), (DOWN_B, 7), (OVER_CORE_B, 6), (OVER_CORE_A, 7), (PARTNER_B, 0), (OVER_CORE_B, 7),
 )
 
 ALONG_X = {"x2": (2,), "zx1": (1,), "zx2": (2,), "zx3": (3,), "mixA": (1, 3), "mixB": (1, 3), "zmixA": (1, 3), "zmixB": (1, 3)}
@@ -416,17 +419,18 @@
     send(tok, T.at[CHUNKS.index("own"), core], own_key, to_core)
     send(tok, T.at[CHUNKS.index("z"), core], z_key, to_zl)
 
-    steps = dict(
-        send_far=send_far, send_near=send_near, forward=forward, gate_up=gate_up, near_sums=near_sums, relay=relay, over_y=over_y,
-        hidden=hidden, near=near, far=far, down=down, over_core=over_core, partner_a=lambda _: partner(0), partner_b=lambda _: partner(1),
-        relay_a=lambda c: relay(c, 0), relay_b=lambda c: relay(c, 1),
-        over_y_a=lambda c: over_y(c, 0), over_y_b=lambda c: over_y(c, 1),
-        hidden_a=lambda c: hidden(c, 0), hidden_b=lambda c: hidden(c, 1),
-        pass_on=pass_on, pass_on_a=lambda c: pass_on(c, 0), pass_on_b=lambda c: pass_on(c, 1),
-        down_first=down_first, down_a=lambda c: down_rest(c, 0), down_b=lambda c: down_rest(c, 1),
-        over_core_a=lambda c: add_cores(c, pl.ds(0, 1024), (0,)),
-        over_core_b=lambda c: add_cores(c, pl.ds(1024, 1024), (1,)),
-    )
+    steps = {
+        SEND_FAR: send_far, SEND_NEAR: send_near, FORWARD: forward, GATE_UP: gate_up, NEAR_SUMS: near_sums,
+        RELAY: relay, RELAY_A: lambda c: relay(c, 0), RELAY_B: lambda c: relay(c, 1),
+        OVER_Y: over_y, OVER_Y_A: lambda c: over_y(c, 0), OVER_Y_B: lambda c: over_y(c, 1),
+        HIDDEN: hidden, HIDDEN_A: lambda c: hidden(c, 0), HIDDEN_B: lambda c: hidden(c, 1),
+        NEAR: near, FAR: far, PASS_ON: pass_on, PASS_ON_A: lambda c: pass_on(c, 0), PASS_ON_B: lambda c: pass_on(c, 1),
+        DOWN: down, DOWN_FIRST: down_first, DOWN_A: lambda c: down_rest(c, 0), DOWN_B: lambda c: down_rest(c, 1),
+        OVER_CORE: over_core,
+        OVER_CORE_A: lambda c: add_cores(c, pl.ds(0, 1024), (0,)),
+        OVER_CORE_B: lambda c: add_cores(c, pl.ds(1024, 1024), (1,)),
+        PARTNER_A: lambda _: partner(0), PARTNER_B: lambda _: partner(1),
+    }
     for name, c in ORDER:
         steps[name](c)
 

time: 101 us -> 101 us (level)
  no operation moved by 1% of the time
where the time goes in v5:
time: 101 us
  Pallas kernels  100 us (99%)
    pallas_call x1, Pallas kernels, on_device(): pl.pallas_call(body, name='gated_layer', out_shape=pltpu.VMEM((64, M), BF...  100 us

profile of v5, /device:TPU:1, one launch (start us, length us, event | category | flops | bytes accessed | tf_op | source)
XLA Modules:
  0.0 100.9 jit_solution(15275804496761982130)
XLA Ops:
  0.0 100.2 %gated_layer.1 = bf16[64,2048]{1,0:T(8,128)(2,1)S(1)} custom-call(bf16[64,2048]{1,0:T(8,128)(2,1)} %tok.1, bf16[2048,1664]{1,0:T(8,128)(2,1)} %wg.1, bf16[2048,1664]{1,0:T(8,128)(2,1)} %wu.1, f32[1664]{0:T(1024)} %gs_in.1, f32[1664]{0:T(1024)} %us_in.1, bf16[1664,2048]{1,0:T(8,128)(2,1)} %wd.1, f32[2048]{0:T(1024)} %ds_in.1), custom_call_target="tpu_custom_call" | custom-call | flops 20937965568 | bytes 20447232 | tf_op jit(solution)/shard_map/gated_layer/pallas_call | solution.py:457
  100.2 0.7 copy.9

commit v6 on v5

--- a/solution.py
+++ b/solution.py
@@ -123,6 +123,8 @@
     for p in partners:
         pl.semaphore_signal(barrier, inc=1, device_id=p, device_id_type=MESH)
     pl.semaphore_wait(barrier, len(partners))
+    own_copy.wait()
+    mine = T.at[CHUNKS.index("own"), core]
 
     def chunk_tokens(c):
         name = CHUNKS[c]
@@ -131,7 +133,7 @@
         return [(T.at[c, core], ("tok", name))]
 
     def send_far(_):
-        send(tok, T.at[CHUNKS.index("x2"), core], ("tok", "x2"), to_x[2])
+        send(mine, T.at[CHUNKS.index("x2"), core], ("tok", "x2"), to_x[2])
 
     def mixed(rows, name):
         c = CHUNKS.index(name)
@@ -140,8 +142,8 @@
         send(rows, T.at[c, core, pl.ds(0, 32)], ("tok", name, 1), to_x[3])
 
     def send_near(_):
-        mixed(tok, "mixA")
-        mixed(tok, "mixB")
+        mixed(mine, "mixA")
+        mixed(mine, "mixB")
 
     def forward(c):
         for where, key in chunk_tokens(c):
@@ -155,8 +157,6 @@
                     mixed(T.at[c, core], name)
 
     def gate_up(c):
-        if CHUNKS[c] == "own":
-            own_copy.wait()
         arrived(T.at[c, other], ("fwd", c))
 
         def tile(n0, width):
@@ -416,8 +416,8 @@
         send(ZLB.at[rows], ZLR.at[rows], ("z_lo", i), to_zl)
 
     own_key, z_key = ("fwd", CHUNKS.index("own")), ("tok", "z")
-    send(tok, T.at[CHUNKS.index("own"), core], own_key, to_core)
-    send(tok, T.at[CHUNKS.index("z"), core], z_key, to_zl)
+    send(mine, T.at[CHUNKS.index("own"), core], own_key, to_core)
+    send(mine, T.at[CHUNKS.index("z"), core], z_key, to_zl)
 
     steps = {
         SEND_FAR: send_far, SEND_NEAR: send_near, FORWARD: forward, GATE_UP: gate_up, NEAR_SUMS: near_sums,

time: 101 us -> 101 us (level)
  no operation moved by 1% of the time
where the time goes in v6:
time: 101 us
  Pallas kernels  100 us (99%)
    pallas_call x1, Pallas kernels, on_device(): pl.pallas_call(body, name='gated_layer', out_shape=pltpu.VMEM((64, M), BF...  100 us

profile of v6, /device:TPU:1, one launch (start us, length us, event | category | flops | bytes accessed | tf_op | source)
XLA Modules:
  0.0 100.7 jit_solution(5749645811262065427)
XLA Ops:
  0.0 100.0 %gated_layer.1 = bf16[64,2048]{1,0:T(8,128)(2,1)S(1)} custom-call(bf16[64,2048]{1,0:T(8,128)(2,1)} %tok.1, bf16[2048,1664]{1,0:T(8,128)(2,1)} %wg.1, bf16[2048,1664]{1,0:T(8,128)(2,1)} %wu.1, f32[1664]{0:T(1024)} %gs_in.1, f32[1664]{0:T(1024)} %us_in.1, bf16[1664,2048]{1,0:T(8,128)(2,1)} %wd.1, f32[2048]{0:T(1024)} %ds_in.1), custom_call_target="tpu_custom_call" | custom-call | flops 20937965568 | bytes 20447232 | tf_op jit(solution)/shard_map/gated_layer/pallas_call | solution.py:457
  100.0 0.7 copy.9
